TPU v7x, 256 devices: a whole 4x4x8 slice. The times are simulated.
256 devices in a mesh: tm: 16 (over y_lo, x, core), space: 16 (over y_hi, z).
Axes of the slice: x: 4, y: 4 (y_hi: 2, y_lo: 2; y = y_hi * 2 + y_lo), z: 8, core: 2. Of those that a mesh axis runs over, the one named last changes fastest.
Arguments:
- eigvecs: bfloat16 [16, 2, 3, 128, 36864], P('tm', None, None, None, 'space'), may hold values from -0.625 to 0.625
- links: bfloat16 [16, 3, 2, 3, 3, 36864], P('tm', None, None, None, None, 'space'), may hold values from -6 to 6
- perambulators: bfloat16 [16, 2, 2, 512, 512], P('tm'), may hold values from -0.03125 to 0.03125
- directions: int32 [4], replicated, may hold values from 0 to 3, each once
- mom_pick: int32 [4], replicated, may hold values from 0 to 6
- mom_table: int32 [7, 3], replicated, may hold values from -2 to 2
Outputs:
- elementals: float32 [4, 2, 16, 128, 128], P(None, None, 'tm', 'space')
- correlators: float32 [2, 16, 2, 4, 4], P(None, 'tm')
Inputs may be any that keep to these rules, and one draw needn't show every extreme that they name: `directions`: each of the four displacement paths is used by exactly one operator.
All inputs are finite; a program needn't handle non-finite values.
Results may differ from a plain program's by a relative error of at most 0.0064.
Values may be sent and summed in bfloat16 or wider, within the bound.
A program may use at most 128 MiB of HBM per device.

v0:
```python
import math

import jax
import jax.numpy as jnp
from jax import lax
from jax.sharding import PartitionSpec as P

LXY = 48
NDT = 1


def shifted(x, axis, by):
    length = lax.axis_size(axis)
    return lax.ppermute(x, axis, [(i, (i + by) % length) for i in range(length)])


def apply_link(link_re, link_im, vec_re, vec_im):
    out_re = 0.0
    out_im = 0.0
    for column in range(3):
        left_re = link_re[:, column][:, None, :]
        left_im = link_im[:, column][:, None, :]
        out_re = out_re + left_re * vec_re[column][None] - left_im * vec_im[column][None]
        out_im = out_im + left_re * vec_im[column][None] + left_im * vec_re[column][None]
    return (out_re, out_im)


def apply_dagger(link_re, link_im, vec_re, vec_im):
    out_re = 0.0
    out_im = 0.0
    for column in range(3):
        left_re = link_re[column][:, None, :]
        left_im = link_im[column][:, None, :]
        out_re = out_re + left_re * vec_re[column][None] + left_im * vec_im[column][None]
        out_im = out_im + left_re * vec_im[column][None] - left_im * vec_re[column][None]
    return (out_re, out_im)


def trace_pairs(x_re, x_im, z_re, z_im):
    high = lax.Precision.HIGHEST
    form = "orc,qrc->oq"
    corr_re = jnp.einsum(form, x_re, z_re, precision=high) - jnp.einsum(
        form, x_im, z_im, precision=high
    )
    corr_im = jnp.einsum(form, x_re, z_im, precision=high) + jnp.einsum(
        form, x_im, z_re, precision=high
    )
    return jnp.stack([corr_re, corr_im])


def contract_columns(tile, sink_elem, source_elem, gamma_sign, col_start, col_count):
    vector_count = sink_elem.shape[-1]
    spin_width = 4 * vector_count
    count = sink_elem.shape[0]
    spin_block = col_start // vector_count
    row_start = col_start % vector_count
    tile_cols = lax.dynamic_slice_in_dim(tile, col_start, col_count, 2)
    tile_block = lax.dynamic_slice_in_dim(tile, spin_block * vector_count, vector_count, 2)
    source_rows = lax.dynamic_slice_in_dim(source_elem, row_start, col_count, 2)

    def left_product(elem, block):
        return jnp.einsum(
            "okl,blc->obkc",
            elem,
            block.reshape(4, vector_count, col_count),
            preferred_element_type=jnp.float32,
        ).reshape(count, spin_width, col_count)

    def right_product(block, elem):
        return jnp.einsum("rl,qkl->qrk", block, elem, preferred_element_type=jnp.float32)

    x_re = left_product(sink_elem[:, 0], tile_cols[0]) - left_product(sink_elem[:, 1], tile_cols[1])
    x_im = left_product(sink_elem[:, 0], tile_cols[1]) + left_product(sink_elem[:, 1], tile_cols[0])
    z_re = (
        right_product(tile_block[0], source_rows[:, 0])
        + right_product(tile_block[1], source_rows[:, 1])
    ) * gamma_sign[None, :, None]
    z_im = (
        right_product(tile_block[0], source_rows[:, 1])
        - right_product(tile_block[1], source_rows[:, 0])
    ) * gamma_sign[None, :, None]
    return trace_pairs(x_re, x_im, z_re, z_im)


def body(eigvecs, links, perambulators, directions, mom_pick, mom_table):
    vectors = eigvecs[0]
    gauge_field = links[0]
    vector_count = vectors.shape[2]
    site_count = vectors.shape[3]
    planes = site_count // (LXY * LXY)
    space_count = lax.axis_size("space")
    space_index = lax.axis_index("space")

    def to_grid(values):
        return values.reshape(values.shape[:-1] + (planes, LXY, LXY))

    def to_flat(values):
        return values.reshape(values.shape[:-3] + (site_count,))

    site_index = jnp.arange(site_count, dtype=jnp.int32)
    coord_x = (site_index % LXY).astype(jnp.float32)
    coord_y = (site_index // LXY % LXY).astype(jnp.float32)
    coord_z = (site_index // (LXY * LXY) + space_index * planes).astype(jnp.float32)
    extent_z = planes * space_count
    momenta = jnp.take(mom_table, mom_pick, axis=0).astype(jnp.float32)
    phase_angle = (
        2.0
        * math.pi
        * (
            momenta[:, 0:1] * coord_x[None] / LXY
            + momenta[:, 1:2] * coord_y[None] / LXY
            + momenta[:, 2:3] * coord_z[None] / extent_z
        )
    )
    path_ids = jnp.arange(4, dtype=jnp.int32)
    matches = (directions[:, None] == path_ids[None, :]).astype(jnp.int32)
    inverse = jnp.sum(matches * path_ids[:, None], axis=0)
    path_angle = jnp.take(phase_angle, inverse, axis=0)
    path_cos = jnp.cos(path_angle)[:, None, None, :]
    path_sin = jnp.sin(path_angle)[:, None, None, :]
    form = "ckn,cln->kl"

    def path_elementals(cand_re, cand_im, which):
        phased_re = (path_cos[which] * cand_re + path_sin[which] * cand_im).astype(jnp.bfloat16)
        phased_im = (path_cos[which] * cand_im - path_sin[which] * cand_re).astype(jnp.bfloat16)
        elem_re = jnp.einsum(
            form, vectors[0], phased_re, preferred_element_type=jnp.float32
        ) + jnp.einsum(form, vectors[1], phased_im, preferred_element_type=jnp.float32)
        elem_im = jnp.einsum(
            form, vectors[0], phased_im, preferred_element_type=jnp.float32
        ) - jnp.einsum(form, vectors[1], phased_re, preferred_element_type=jnp.float32)
        return jnp.stack([elem_re, elem_im])

    vec_f = vectors.astype(jnp.float32)
    vec_grid = to_grid(vectors)
    upper_plane = shifted(vec_grid, "space", -1)
    ahead_z = to_flat(jnp.concatenate([vec_grid[..., 1:, :, :], upper_plane], axis=-3))
    path_results = [path_elementals(vec_f[0], vec_f[1], 0)]
    for direction in range(3):
        link_re = gauge_field[direction, 0].astype(jnp.float32)
        link_im = gauge_field[direction, 1].astype(jnp.float32)
        back_re, back_im = apply_dagger(link_re, link_im, vec_f[0], vec_f[1])
        back_all = lax.optimization_barrier(jnp.stack([back_re, back_im]).astype(jnp.bfloat16))
        if direction < 2:
            axis_pos = -1 - direction
            ahead = to_flat(jnp.roll(vec_grid, -1, axis_pos))
            behind = to_flat(jnp.roll(to_grid(back_all), 1, axis_pos))
        else:
            back_grid = to_grid(back_all)
            lower_plane = shifted(back_grid, "space", 1)
            ahead = ahead_z
            behind = to_flat(
                jnp.concatenate([lower_plane, back_grid[..., : planes - 1, :, :]], axis=-3)
            )
        ahead = ahead.astype(jnp.float32)
        behind = behind.astype(jnp.float32)
        fwd_re, fwd_im = apply_link(link_re, link_im, ahead[0], ahead[1])
        path_results.append(path_elementals(fwd_re - behind[0], fwd_im - behind[1], direction + 1))
    partial_elem = jnp.take(jnp.stack(path_results), directions, axis=0)
    row_count = vector_count // space_count
    total = lax.psum(partial_elem, "space")
    own_rows = lax.dynamic_slice_in_dim(total, space_index * row_count, row_count, 2)
    rounded = total.astype(jnp.bfloat16)
    source_list = []
    distance = 1
    source_list.append(shifted(rounded, "tm", distance))
    distance = 1
    source_list.append(shifted(rounded, "tm", -distance))
    gamma_sign = jnp.where(
        jnp.arange(4 * vector_count, dtype=jnp.int32) // vector_count < 2, 1.0, -1.0
    ).astype(jnp.float32)
    results = []
    col_count = 4 * vector_count // space_count
    col_start = space_index * col_count
    for offset in range(2 * NDT):
        results.append(
            contract_columns(
                perambulators[0, offset],
                rounded,
                source_list[offset],
                gamma_sign,
                col_start,
                col_count,
            )
        )
    corr = lax.psum(jnp.stack(results, axis=1), "space")
    return (own_rows[:, :, None], corr[:, None])


def solution(mesh):
    placed = (
        P("tm", None, None, None, "space"),
        P("tm", None, None, None, None, "space"),
        P("tm", None, None, None, None),
        P(),
        P(),
        P(),
    )
    return jax.shard_map(
        body,
        mesh=mesh,
        in_specs=placed,
        out_specs=(P(None, None, "tm", "space", None), P(None, "tm", None, None, None)),
        check_vma=False,
    )
```

profile of v0, /device:TPU:2, one launch (start us, length us, event | category | flops | bytes accessed | tf_op | source)
XLA Modules:
  0.0 417.4 jit_solution(358728163060555342)
XLA Ops:
  7.2 2.2 slice_convert_fusion.5
  13.2 5.8 %fusion.216 = (f32[1,2,3,128,2304]{4,3,2,1,0:T(8,128)}, f32[2,3,128,2304]{3,2,1,0:T(8,128)S(1)}) fusion(bf16[1,2,3,128,2304]{4,3,2,1,0:T(8,128)(2,1)} %param.6), kind=kLoop, calls=%fused_computation.338 | loop fusion | flops 1769472 | bytes 17694720 | tf_op jit(solution)/shard_map/convert_element_type | solution.py:134
  19.1 2.5 slice_bitcast_fusion.19
  22.3 2.1 copy.112
  24.4 3.1 copy.111
  27.5 2.7 copy.110
  30.1 2.7 copy.109
  32.8 9.6 %add_convert_fusion.1 = (bf16[1,3,128,2304]{2,3,1,0:T(8,128)(2,1)S(1)}, bf16[1,3,128,2304]{2,3,1,0:T(8,128)(2,1)S(1)}) fusion(f32[3,2304]{1,0:T(4,128)} %bitcast.662, f32[3,2304]{1,0:T(4,128)} %bitcast.663, f32[3,2304]{1,0:T(4,128)} %bitcast.665, f32[3,2304]{1,0:T(4,128)} %bitcast.666, f32[3,2304]{1,0:T(4,128)} %bitcast.667, f32[3,2304]{1,0:T(4,128)} %bitcast.668, ...), kind=kLoop, calls=%fused_computation.16 | loop fusion | flops 21233664 | bytes 10782720 | tf_op jit(solution)/shard_map/convert.3
  42.5 2.2 pad_maximum_fusion.4
  46.6 4.6 %copy.108 = bf16[1,2,3,128,2304]{3,4,2,1,0:T(8,128)(2,1)S(1)} copy(bf16[1,2,3,128,2304]{4,3,2,1,0:T(8,128)(2,1)} %param.6) | data formatting | bytes 7077888 | tf_op args[0]
  51.2 6.8 %collective-permute-start = (bf16[2,3,128,1,48,48]{2,5,4,1,0,3:T(8,128)(2,1)S(1)}, bf16[2,3,128,1,48,48]{2,5,4,1,0,3:T(8,128)(2,1)}, u32[]{:S(2)}, u32[]{:S(2)}) collective-permute-start(bf16[2,3,128,1,48,48]{2,5,4,1,0,3:T(8,128)(2,1)S(1)} %bitcast.625), channel_id=1, source_target_pairs={{0,15},{1,0},{2,1},{3,2},{4,3},{5,4},{6,5},{7,6},{8,7},{9,8},{10,9... | collective-permute-start | bytes 10616840 | tf_op jit(solution)/shard_map/ppermute | solution.py:14
  64.8 15.0 %add_convert_fusion.5 = (bf16[1,3,128,2304]{2,3,1,0:T(8,128)(2,1)}, bf16[1,3,128,2304]{2,3,1,0:T(8,128)(2,1)}, bf16[1,3,128,2304]{2,3,1,0:T(8,128)(2,1)S(1)}, bf16[1,3,128,2304]{2,3,1,0:T(8,128)(2,1)S(1)}) fusion(f32[128,2304]{0,1:T(8,128)} %copy-done.4, f32[3,2304]{1,0:T(4,128)S(1)} %bitcast.657, f32[128,2304]{0,1:T(8,128)} %copy-done.5, ...), kind=kLoop, calls=%fused_computation.28 | loop fusion | flops 42467328 | bytes 14487552 | tf_op jit(solution)/shard_map/convert.7
  80.2 2.4 slice.736
  83.8 2.4 slice.715
  87.7 3.8 slice.681
  105.3 2.4 maximum_convert_fusion.1
  111.7 6.9 %fusion.4 = (bf16[3,128,2304]{1,2,0:T(8,128)(2,1)S(1)}, f32[1,3,128,2304]{2,3,1,0:T(8,128)S(1)}, f32[1,3,128,2304]{2,3,1,0:T(8,128)S(1)}) fusion(f32[2304]{0:T(1024)S(1)} %get-tuple-element.14, f32[2304]{0:T(1024)S(1)} %get-tuple-element.10, f32[1,3,128,2304]{2,3,1,0:T(8,128)S(1)} %bitcast.633, f32[128,2304]{0,1:T(8,128)S(1)} %get-tuple-element.50, ...), kind=kLoop, calls=%fused_computation.36 | loop fusion | flops 24772608 | bytes 23187456 | tf_op jit(solution)/shard_map/convert_element_type | solution.py:124
  130.6 6.9 %fusion.2 = (bf16[3,128,2304]{1,2,0:T(8,128)(2,1)S(1)}, f32[1,3,128,2304]{2,3,1,0:T(8,128)S(1)}, f32[1,3,128,2304]{2,3,1,0:T(8,128)S(1)}) fusion(f32[2304]{0:T(1024)S(1)} %get-tuple-element.15, f32[2304]{0:T(1024)S(1)} %get-tuple-element.11, f32[1,3,128,2304]{2,3,1,0:T(8,128)S(1)} %bitcast.635, f32[128,2304]{0,1:T(8,128)S(1)} %get-tuple-element.40, ...), kind=kLoop, calls=%fused_computation.34 | loop fusion | flops 24772608 | bytes 23187456 | tf_op jit(solution)/shard_map/convert_element_type | solution.py:124
  153.6 4.1 fusion
  160.8 2.5 convert.29
  163.8 2.5 fusion.217
  166.4 6.9 %fusion.6 = (bf16[3,128,2304]{1,2,0:T(8,128)(2,1)S(1)}, f32[1,3,128,2304]{2,3,1,0:T(8,128)S(1)}, f32[1,3,128,2304]{2,3,1,0:T(8,128)S(1)}) fusion(f32[2304]{0:T(1024)S(1)} %get-tuple-element.13, f32[2304]{0:T(1024)S(1)} %copy-done.31, f32[1,3,128,2304]{2,3,1,0:T(8,128)S(1)} %bitcast.637, f32[128,2304]{0,1:T(8,128)S(1)} %get-tuple-element.56, ...), kind=kLoop, calls=%fused_computation.38 | loop fusion | flops 24772608 | bytes 23187456 | tf_op jit(solution)/shard_map/convert_element_type | solution.py:124
  180.9 152.6 %all-reduce.2.cloned.1.call-done = f32[4,2,128,128]{2,3,1,0:T(8,128)} async-done(((f32[4,2,128,128]{2,3,1,0:T(8,128)}), f32[4,2,128,128]{2,3,1,0:T(8,128)}) %all-reduce.2.cloned.1.call-update) | async-done | bytes 524304 | tf_op jit(solution)/shard_map/psum | solution.py:161
  368.4 42.0 %psum.15 = f32[2,1,2,4,4]{4,3,2,0,1:T(4,128)} all-reduce(f32[2,1,2,4,4]{4,3,2,0,1:T(4,128)S(1)} %copy_bitcast_fusion.42), channel_id=1, replica_groups=mesh['tm'=16,'space'=16] {'space'}, use_global_device_ids=true, to_apply=%region_2.3 | all-reduce | flops 64 | bytes 512 | tf_op jit(solution)/shard_map/psum | solution.py:186
  (233 shorter events, 107.5 us)
Async XLA Ops:
  7.2 326.3 %all-reduce.2.cloned.1.call-start = ((), (), s32[]{:S(2)}) async-start(), calls=%async_computation | async-start | bytes 1048576 | tf_op jit(solution)/shard_map/psum | solution.py:161
  9.4 9.6 %copy-start.15 = (f32[1,1,3,3,2304]{4,1,3,2,0:T(1,128)}, f32[1,1,3,3,2304]{4,1,3,2,0:T(1,128)S(1)}, u32[]{:S(2)}) copy-start(f32[1,1,3,3,2304]{4,1,3,2,0:T(1,128)S(1)} %get-tuple-element.77) | copy-start | bytes 248836
  9.4 9.6 %copy-start.16 = (f32[1,1,3,3,2304]{4,1,3,2,0:T(1,128)}, f32[1,1,3,3,2304]{4,1,3,2,0:T(1,128)S(1)}, u32[]{:S(2)}) copy-start(f32[1,1,3,3,2304]{4,1,3,2,0:T(1,128)S(1)} %get-tuple-element.78) | copy-start | bytes 248836
  21.9 11.0 %copy-start.4 = (f32[128,2304]{0,1:T(8,128)}, f32[128,2304]{0,1:T(8,128)S(1)}, u32[]{:S(2)}) copy-start(f32[128,2304]{0,1:T(8,128)S(1)} %copy.114) | copy-start | bytes 3538948
  22.3 10.6 %copy-start.5 = (f32[128,2304]{0,1:T(8,128)}, f32[128,2304]{0,1:T(8,128)S(1)}, u32[]{:S(2)}) copy-start(f32[128,2304]{0,1:T(8,128)S(1)} %copy.113) | copy-start | bytes 3538948
  24.4 8.5 %copy-start.6 = (f32[128,2304]{0,1:T(8,128)}, f32[128,2304]{0,1:T(8,128)S(1)}, u32[]{:S(2)}) copy-start(f32[128,2304]{0,1:T(8,128)S(1)} %copy.112) | copy-start | bytes 3538948
  44.7 14.2 %copy-start.33 = (s32[4]{0:T(128)S(1)}, s32[4]{0:T(128)}, u32[]{:S(2)}) copy-start(s32[4]{0:T(128)} %param.10) | copy-start | bytes 52
  44.7 119.1 %collective-permute-start.1 = (bf16[2,3,128,1,48,48]{2,5,4,1,0,3:T(8,128)(2,1)}, bf16[2,3,128,1,48,48]{2,5,4,1,0,3:T(8,128)(2,1)}, u32[]{:S(2)}, u32[]{:S(2)}) collective-permute-start(bf16[2,3,128,1,48,48]{2,5,4,1,0,3:T(8,128)(2,1)} %bitcast.78), channel_id=1, source_target_pairs={{0,1},{1,2},{2,3},{3,4},{4,5},{5,6},{6,7},{7,8},{8,9},{9,10},{10,1... | collective-permute-start | bytes 10616840 | tf_op jit(solution)/shard_map/ppermute | solution.py:14
  51.2 109.5 %collective-permute-start = (bf16[2,3,128,1,48,48]{2,5,4,1,0,3:T(8,128)(2,1)S(1)}, bf16[2,3,128,1,48,48]{2,5,4,1,0,3:T(8,128)(2,1)}, u32[]{:S(2)}, u32[]{:S(2)}) collective-permute-start(bf16[2,3,128,1,48,48]{2,5,4,1,0,3:T(8,128)(2,1)S(1)} %bitcast.625), channel_id=1, source_target_pairs={{0,15},{1,0},{2,1},{3,2},{4,3},{5,4},{6,5},{7,6},{8,7},{9,8},{10,9... | collective-permute-start | bytes 10616840 | tf_op jit(solution)/shard_map/ppermute | solution.py:14
  83.1 3.0 copy-start.13
  83.1 3.0 copy-start.14
  87.7 3.8 copy-start.11
  87.7 3.8 copy-start.12
  140.5 3.2 copy-start.19
  140.5 3.9 copy-start.32
  153.6 4.1 copy-start.2
  163.7 2.6 copy-start.25
  163.7 2.6 copy-start.26
  163.7 2.6 copy-start.27
  163.8 2.6 copy-start.28
  333.5 6.2 %copy-start.9 = (f32[4,2,128,128]{2,3,1,0:T(8,128)S(1)}, f32[4,2,128,128]{2,3,1,0:T(8,128)}, u32[]{:S(2)}) copy-start(f32[4,2,128,128]{2,3,1,0:T(8,128)} %all-reduce.2.cloned.1.call-done) | copy-start | bytes 1572868
  334.6 13.7 %collective-permute-start.3 = (bf16[4,2,128,128]{2,3,1,0:T(8,128)(2,1)S(1)}, bf16[4,2,128,128]{2,3,1,0:T(8,128)(2,1)}, u32[]{:S(2)}, u32[]{:S(2)}) collective-permute-start(bf16[4,2,128,128]{2,3,1,0:T(8,128)(2,1)S(1)} %convert_element_type.202), channel_id=1, source_target_pairs={{0,240},{16,0},{32,16},{48,32},{64,48},{80,64},{96,80},{112,96},{1... | collective-permute-start | bytes 786440 | tf_op jit(solution)/shard_map/ppermute | solution.py:14
  334.9 23.5 %collective-permute-start.2 = (bf16[4,2,128,128]{2,3,1,0:T(8,128)(2,1)S(1)}, bf16[4,2,128,128]{2,3,1,0:T(8,128)(2,1)}, u32[]{:S(2)}, u32[]{:S(2)}) collective-permute-start(bf16[4,2,128,128]{2,3,1,0:T(8,128)(2,1)S(1)} %convert_element_type.202), channel_id=1, source_target_pairs={{0,16},{16,32},{32,48},{48,64},{64,80},{80,96},{96,112},{112,128},... | collective-permute-start | bytes 786440 | tf_op jit(solution)/shard_map/ppermute | solution.py:14
  339.9 6.3 %copy-start.10 = (f32[4,32,4,128]{3,1,2,0:T(8,128)S(1)}, f32[4,32,4,128]{3,1,2,0:T(8,128)}, u32[]{:S(2)}) copy-start(f32[4,32,4,128]{3,1,2,0:T(8,128)} %fusion.187) | copy-start | bytes 786436
  (17 other events, 29.1 us)
Sparse Core Ops, SparseCore 0:
  179.1 154.3 all-reduce.1
where the time goes:
time: 424 us; the launch traced here: 417 us
  waiting for transfers between devices  153 us (36%)
  other arithmetic  86.5 us (20%)
  local copies, waits for them, and re-layouts  75.1 us (18%)
  blocking collectives  42 us (10%)
  matrix products  36.3 us (9%)
  between operations  15.3 us (4%)
  starting transfers between devices  9.54 us (2%)
    psum x1, waiting for transfers between devices, body(): total = lax.psum(partial_elem, 'space')  153 us
    psum x1, blocking collectives, body(): corr = lax.psum(jnp.stack(results, axis=1), 'space')  42 us
    unnamed x114, local copies, waits for them, and re-layouts  25.9 us
    convert_element_type x4, other arithmetic, path_elementals(): (path_cos[which] * cand_re + path_sin[which] * cand_im).astype(jnp.bfloat16)  24.7 us
    another operation x2, other arithmetic  24.6 us
    dot_general x8, matrix products, right_product(): jnp.einsum('rl,qkl->qrk', block, elem, preferred_element_type=jnp.float32)  9.7 us
    ppermute x4, starting transfers between devices, shifted(): lax.ppermute(x, axis, [(i, (i + by) % length) for i in range(length)])  9.5 us
    mul x4, local copies, waits for them, and re-layouts, apply_dagger(): left_re * vec_re[column][None]  8.61 us
  transfers between devices with their start and end apart: 5, of which 1 were waited for; matrix products, arithmetic and copies ran while one was open for 31% of the time, Pallas kernels for 0%

commit v1 on v0

v1 whole, which is shorter than its diff:
```python
import functools
import math

import jax
import jax.numpy as jnp
from jax import lax
from jax.experimental import pallas as pl
from jax.experimental.pallas import tpu as pltpu
from jax.sharding import PartitionSpec as P

LXY = 48
MESH = pl.DeviceIdType.MESH
F32 = jnp.float32
BF16 = jnp.bfloat16
NT = (((1,), (1,)), ((), ()))
LANES = 128
HALF = 9
BLOCKS = 18
NV = 128
ROWS = 8


def dot_nt(a, b):
    return lax.dot_general(a, b, NT, preferred_element_type=F32)


def kernel(n_tm, n_space, eig, links, tau, dirs, pick, table, elem_out, corr_out,
           vbuf, rdn, rup, lk, lkup, lkf, lkupf, ph, lhs, rhs, acc0, accd, part,
           rs_send, rs_recv, own, ag_send, ag, tauo, taun, zbuf, wmat, rowbuf,
           ps_send, ps_own, ps_even, local_sem, halo_send, halo_recv, lk_sem, tau_sem,
           rs_sem, ag_sem, ps_sem, go_sem):
    t = lax.axis_index("tm")
    me = lax.axis_index("space")
    odd = lax.rem(t, 2) == 1
    even = lax.rem(t, 2) == 0
    t_next = lax.rem(t + 1, n_tm)
    t_prev = lax.rem(t + n_tm - 1, n_tm)
    up = lax.rem(me + 1, n_space)
    down = lax.rem(me + n_space - 1, n_space)

    def dev(a, b):
        return {"tm": a, "space": b}

    def remote(src, dst, ssem, rsem, where):
        return pltpu.make_async_remote_copy(
            src_ref=src, dst_ref=dst, send_sem=ssem, recv_sem=rsem,
            device_id=where, device_id_type=MESH)

    def wait_bytes(ref, sem):
        pltpu.make_async_copy(ref, ref, sem).wait()

    def load_block(j):
        return pltpu.make_async_copy(
            eig.at[0, :, :, :, pl.ds(pl.multiple_of(j * LANES, LANES), LANES)],
            vbuf.at[j], local_sem.at[0])

    pltpu.make_async_copy(links.at[0], lk, local_sem.at[1]).start()

    def start_load(j, carry):
        load_block(j).start()
        return carry

    lax.fori_loop(0, BLOCKS, start_load, 0)
    pltpu.make_async_copy(tau.at[0], tauo, local_sem.at[2]).start()

    barrier = pltpu.get_barrier_semaphore()

    def greet(a, b):
        pl.semaphore_signal(barrier, inc=1, device_id=dev(a, b), device_id_type=MESH)

    greet(t, up)
    greet(t, down)

    def greet_group(k, carry):
        greet(t, lax.rem(me + k, n_space))
        return carry

    lax.fori_loop(2, n_space - 1, greet_group, 0)

    def greet_near(k, carry):
        greet(t_next, k)
        greet(t_prev, k)
        return carry

    lax.fori_loop(0, n_space, greet_near, 0)
    pl.semaphore_wait(barrier, 3 * n_space - 1)

    def halo(n, side):
        j = n + HALF * side
        return remote(
            eig.at[0, :, :, :, pl.ds(pl.multiple_of(j * LANES, LANES), LANES)],
            (rup if side else rdn).at[n], halo_send.at[side, n], halo_recv.at[side, n],
            dev(t, up if side else down))

    def start_halo(n, carry):
        halo(n, 0).start()
        halo(n, 1).start()
        return carry

    link_copy = remote(links.at[0, 2, :, :, :, pl.ds(HALF * LANES, HALF * LANES)], lkup,
                       lk_sem.at[0], lk_sem.at[1], dev(t, up))
    link_copy.start()

    @pl.when(even)
    def _():
        lax.fori_loop(0, HALF, start_halo, 0)
        remote(tau.at[0, 0], taun.at[0], tau_sem.at[0], tau_sem.at[2], dev(t_prev, me)).start()
        remote(tau.at[0, 1], taun.at[1], tau_sem.at[1], tau_sem.at[3], dev(t_next, me)).start()

    site = (lax.broadcasted_iota(jnp.int32, (24, LANES), 0) * LANES
            + lax.broadcasted_iota(jnp.int32, (24, LANES), 1)).astype(F32)
    site_y = jnp.floor((site + 0.5) * (1.0 / LXY))
    site_x = site - site_y * LXY

    def spread_scalar(value):
        return jnp.full((1, LANES), value, jnp.int32)

    picked = []
    for o in range(4):
        choice = spread_scalar(pick[o])
        row = [jnp.zeros((1, LANES), jnp.int32)] * 3
        for r in range(table.shape[0]):
            row = [jnp.where(choice == r, spread_scalar(table[r, axis]), row[axis]) for axis in range(3)]
        picked.append(row)

    def path_momentum(path, axis):
        total = jnp.zeros((1, LANES), jnp.int32)
        for o in range(4):
            total = jnp.where(spread_scalar(dirs[o]) == path, picked[o][axis], total)
        return total.astype(F32)

    mom = [[path_momentum(path, axis) for axis in range(3)] for path in range(4)]
    extent_z = 1.0 * n_space
    plane = me.astype(F32)
    for path in range(4):
        flat = 2.0 * math.pi * (mom[path][0] * site_x / LXY + mom[path][1] * site_y / LXY
                                + mom[path][2] * plane / extent_z)
        ph[path, 0] = jnp.cos(flat)
        ph[path, 1] = jnp.sin(flat)
    flat = 2.0 * math.pi * (mom[3][0] * site_x / LXY + mom[3][1] * site_y / LXY
                            + mom[3][2] * (plane - 1.0) / extent_z)
    ph[4, 0] = jnp.cos(flat)
    ph[4, 1] = jnp.sin(flat)

    wait_bytes(lk, local_sem.at[1])
    for d in range(3):
        for ri in range(2):
            for c in range(3):
                lkf[d, ri, c] = lk[d, ri, c].astype(F32)
    wait_bytes(vbuf, local_sem.at[0])

    acc0[...] = jnp.zeros_like(acc0)
    accd[...] = jnp.zeros_like(accd)
    lane = lax.broadcasted_iota(jnp.int32, (NV, LANES), 1)

    def link_rows(ref_row):
        return [[[jnp.broadcast_to(ref_row(ri, c, a), (16, LANES)) for a in range(3)]
                 for c in range(3)] for ri in range(2)]

    def back_block(vref, u, cosine, sine, slot):
        cosine = jnp.broadcast_to(cosine, (16, LANES))
        sine = jnp.broadcast_to(sine, (16, LANES))

        def tile(k, carry):
            at = pl.multiple_of(k * 16, 16)
            v = [[vref[ri, c, pl.ds(at, 16), :].astype(F32) for c in range(3)] for ri in range(2)]
            for a in range(3):
                b_re = u[0][0][a] * v[0][0] + u[1][0][a] * v[1][0]
                b_im = u[0][0][a] * v[1][0] - u[1][0][a] * v[0][0]
                for c in (1, 2):
                    b_re = b_re + u[0][c][a] * v[0][c] + u[1][c][a] * v[1][c]
                    b_im = b_im + u[0][c][a] * v[1][c] - u[1][c][a] * v[0][c]
                col = pl.ds((slot * 3 + a) * LANES, LANES)
                lhs[pl.ds(at, 16), col] = (cosine * b_re).astype(BF16)
                lhs[pl.ds(at + 128, 16), col] = (cosine * b_im).astype(BF16)
                lhs[pl.ds(at + 256, 16), col] = (sine * b_re).astype(BF16)
                lhs[pl.ds(at + 384, 16), col] = (sine * b_im).astype(BF16)
            return carry

        lax.fori_loop(0, NV // 16, tile, 0, unroll=2)

    def own_links(d, j):
        at = pl.ds(pl.multiple_of(j * LANES, LANES), LANES)
        return link_rows(lambda ri, c, a: lkf[d, ri, c, a:a + 1, at])

    def plain_block(j, slot):
        cosine = jnp.broadcast_to(ph[0, 0, pl.ds(j, 1), :], (16, LANES))
        sine = jnp.broadcast_to(ph[0, 1, pl.ds(j, 1), :], (16, LANES))

        def tile(k, carry):
            at = pl.multiple_of(k * 16, 16)
            for c in range(3):
                v_re = vbuf[j, 0, c, pl.ds(at, 16), :].astype(F32)
                v_im = vbuf[j, 1, c, pl.ds(at, 16), :].astype(F32)
                col = pl.ds((slot * 3 + c) * LANES, LANES)
                rhs[pl.ds(at, 16), col] = (cosine * v_re + sine * v_im).astype(BF16)
                rhs[pl.ds(at + 128, 16), col] = (cosine * v_im - sine * v_re).astype(BF16)
            return carry

        lax.fori_loop(0, NV // 16, tile, 0, unroll=2)

    def ahead_block(d, j, slot):
        after = jnp.where(j == BLOCKS - 1, 0, j + 1)
        before = jnp.where(j == 0, BLOCKS - 1, j - 1)
        if d == 0:
            edge = lax.rem(j * LANES + lane, LXY) == LXY - 1
        for ri in range(2):
            for c in range(3):
                here = vbuf[j, ri, c]
                there = vbuf[after, ri, c]
                if d == 1:
                    turned = jnp.where(lane < LANES - LXY, pltpu.roll(here, LANES - LXY, 1),
                                       pltpu.roll(there, LANES - LXY, 1))
                else:
                    back = vbuf[before, ri, c]
                    near = jnp.where(lane == LANES - 1, pltpu.roll(there, LANES - 1, 1),
                                     pltpu.roll(here, LANES - 1, 1))
                    far = jnp.where(lane < LXY - 1, pltpu.roll(back, LXY - 1, 1),
                                    pltpu.roll(here, LXY - 1, 1))
                    turned = jnp.where(edge, far, near)
                rhs[pl.ds(ri * 128, 128), pl.ds((slot * 3 + c) * LANES, LANES)] = turned

    def stacked(parts):
        return jnp.concatenate(
            [jnp.concatenate([p[ri, c] for p in parts for c in range(3)], axis=1) for ri in range(2)],
            axis=0)

    def local_pair(i, carry):
        j = 2 * i
        for s in range(2):
            plain_block(j + s, s)
        acc0[...] += dot_nt(stacked([vbuf.at[j], vbuf.at[j + 1]]), rhs[...])
        for d in range(2):
            for s in range(2):
                back_block(vbuf.at[j + s], own_links(d, j + s), ph[d + 1, 0, pl.ds(j + s, 1), :],
                           ph[d + 1, 1, pl.ds(j + s, 1), :], s)
                ahead_block(d, j + s, s)
            accd[d] += dot_nt(lhs[...], rhs[...])
        return carry

    lax.fori_loop(0, BLOCKS // 2, local_pair, 0)

    def blocks_of(ref, row):
        g_rr = ref[row:row + 128, 0:128]
        g_ri = ref[row:row + 128, 128:256]
        g_ir = ref[row + 128:row + 256, 0:128]
        g_ii = ref[row + 128:row + 256, 128:256]
        return g_rr + g_ii, g_ri - g_ir

    def finish_direction(d):
        c_re, c_im = blocks_of(accd.at[d], 0)
        s_re, s_im = blocks_of(accd.at[d], 256)
        length = (float(LXY), float(LXY), extent_z)[d]
        turn = jnp.full((1, LANES), 2.0 * math.pi / length, F32) * mom[d + 1][d]
        cosine = jnp.cos(turn)
        sine = jnp.sin(turn)
        p_re = c_re - s_im
        p_im = c_im + s_re
        n_re = cosine * p_re - sine * p_im
        n_im = sine * p_re + cosine * p_im
        part[d + 1, 0] = c_re + s_im - n_re.T
        part[d + 1, 1] = c_im - s_re + n_im.T

    part[0, 0], part[0, 1] = blocks_of(acc0, 0)
    finish_direction(0)
    finish_direction(1)

    def spread(first, count, which):
        width = 16 * count
        for j in range(n_space):
            for p in range(count):
                for ri in range(2):
                    own[which, pl.ds(p * 16 + ri * 8, 8), :] = part[first + p, ri, j * 8:(j + 1) * 8, :]
            rs_send[which, j, 0:width, :] = own[which, 0:width, :].astype(BF16)
        for p in range(count):
            for ri in range(2):
                own[which, pl.ds(p * 16 + ri * 8, 8), :] = part[
                    first + p, ri, pl.ds(pl.multiple_of(me * 8, 8), 8), :]

        def send(k, carry):
            j = lax.rem(me + k, n_space)
            remote(rs_send.at[which, j, pl.ds(0, width)], rs_recv.at[which, k - 1, pl.ds(0, width)],
                   rs_sem.at[which, 0], rs_sem.at[which, 1], dev(t, j)).start()
            return carry

        lax.fori_loop(1, n_space, send, 0)

    def gather(which, width):
        wait_bytes(rs_recv.at[which, :, pl.ds(0, width)], rs_sem.at[which, 1])
        total = own[which, 0:width, :]
        for k in range(n_space - 1):
            total = total + rs_recv[which, k, 0:width, :].astype(F32)
        own[which, 0:width, :] = total

    def publish(which, width):
        ag_send[which, 0:width, :] = own[which, 0:width, :].astype(BF16)

        def send(j, carry):
            remote(ag_send.at[which, pl.ds(0, width)], ag.at[which, 0, me, pl.ds(0, width)],
                   ag_sem.at[which, 0], ag_sem.at[which, 1], dev(t_next, j)).start()
            remote(ag_send.at[which, pl.ds(0, width)], ag.at[which, 1, me, pl.ds(0, width)],
                   ag_sem.at[which, 0], ag_sem.at[which, 1], dev(t_prev, j)).start()
            return carry

        lax.fori_loop(0, n_space, send, 0)

    spread(0, 3, 0)

    link_copy.wait()
    for ri in range(2):
        for c in range(3):
            lkupf[ri, c] = lkup[ri, c].astype(F32)

    def z_block(n, carry):
        halo(n, 0).wait_recv()
        halo(n, 1).wait_recv()
        at = pl.ds(pl.multiple_of(n * LANES, LANES), LANES)
        back_block(vbuf.at[n], own_links(2, n), ph[3, 0, pl.ds(n, 1), :], ph[3, 1, pl.ds(n, 1), :], 0)
        u = link_rows(lambda ri, c, a: lkupf[ri, c, a:a + 1, at])
        m = n + HALF
        back_block(rup.at[n], u, ph[4, 0, pl.ds(m, 1), :], ph[4, 1, pl.ds(m, 1), :], 1)
        accd[2] += dot_nt(lhs[...], stacked([rdn.at[n], vbuf.at[m]]))
        return carry

    def wait_halo_sends(lo, hi):
        def one(n, carry):
            halo(n, 0).wait_send()
            halo(n, 1).wait_send()
            return carry

        lax.fori_loop(lo, hi, one, 0)

    def weights(kind, e, which, slot, path):
        src = 0 if e == 0 else 1
        if kind == 1:
            src = 1 - e
        re_rows, im_rows = [], []
        at = pl.multiple_of(slot * 16, 16)
        for j in range(n_space):
            both = ag[which, src, j, pl.ds(at, 16), :].astype(F32)
            re_rows.append(both[0:8])
            im_rows.append(both[8:16])
        phi_re = jnp.concatenate(re_rows, axis=0)
        phi_im = jnp.concatenate(im_rows, axis=0)
        if kind == 0:
            first = jnp.concatenate([phi_re, phi_im], axis=1)
            second = jnp.concatenate([phi_im, -phi_re], axis=1)
        else:
            first = jnp.concatenate([phi_re, -phi_im], axis=1)
            second = jnp.concatenate([phi_im, phi_re], axis=1)
        phi = jnp.concatenate([first, second], axis=0).astype(BF16)
        mat = tauo.at[e] if kind == 0 else taun.at[e]
        for c in range(4):
            col = slice(c * 128, (c + 1) * 128)
            z = dot_nt(jnp.concatenate([mat[0, :, col], mat[1, :, col]], axis=1), phi)
            if kind == 1 and c >= 2:
                z = -z
            zbuf[0, :, col] = z[:, 0:128].astype(BF16)
            zbuf[1, :, col] = z[:, 128:256].astype(BF16)
        total = None
        for r in range(4):
            row = slice(r * 128, (r + 1) * 128)
            g = dot_nt(jnp.concatenate([zbuf[0, row, :], zbuf[1, row, :]], axis=0),
                       jnp.concatenate([mat[0, row, :], mat[1, row, :]], axis=0))
            if total is None:
                total = g
            elif kind == 0 and r >= 2:
                total = total - g
            else:
                total = total + g
        rr, ri_, ir, ii = (total[0:128, 0:128], total[0:128, 128:256],
                           total[128:256, 0:128], total[128:256, 128:256])
        if kind == 0:
            wmat[kind, e, path, 0] = rr - ii
            wmat[kind, e, path, 1] = ri_ + ir
        else:
            wmat[kind, e, path, 0] = rr + ii
            wmat[kind, e, path, 1] = ir - ri_

    def weights_of(which, count, first):
        for kind in range(2):
            for e in range(2):
                def one(slot, carry, kind=kind, e=e):
                    weights(kind, e, which, slot, first + slot)
                    return carry

                lax.fori_loop(0, count, one, 0)

    def pair_rows(paths, lo, hi):
        for kind in range(2):
            for e in range(2):
                for p in paths:
                    def one(w, carry, kind=kind, e=e, p=p):
                        w_re, w_im = wmat[kind, e, w, 0], wmat[kind, e, w, 1]
                        p_re, p_im = part[p, 0], part[p, 1]
                        re = jnp.sum(p_re * w_re - p_im * w_im, axis=0, keepdims=True)
                        im = jnp.sum(p_re * w_im + p_im * w_re, axis=0, keepdims=True)
                        if kind == 0:
                            rowbuf[kind, w, pl.ds(e * 4 + p, 1), :] = re
                            rowbuf[kind, w, pl.ds(8 + e * 4 + p, 1), :] = im
                        else:
                            rowbuf[kind, p, pl.ds(e * 4 + w, 1), :] = re
                            rowbuf[kind, p, pl.ds(8 + e * 4 + w, 1), :] = im
                        return carry

                    lax.fori_loop(lo, hi, one, 0)

    def write_elementals():
        for o in range(4):
            path = jnp.full((8, LANES), dirs[o], jnp.int32)
            for ri in range(2):
                rows = own[1, ri * 8:(ri + 1) * 8, :]
                for p in range(3):
                    rows = jnp.where(path == p, own[0, p * 16 + ri * 8:p * 16 + ri * 8 + 8, :], rows)
                elem_out[o, ri, 0] = rows

    def write_correlators(total):
        col = lax.broadcasted_iota(jnp.int32, (16, LANES), 1)
        turned = jnp.zeros((16, LANES), F32)
        for q in range(4):
            one = jnp.sum(jnp.where(col == spread_scalar(dirs[q]), total, 0.0), axis=1, keepdims=True)
            turned = jnp.where(col == q, one, turned)
        for o in range(4):
            path = jnp.full((1, LANES), dirs[o], jnp.int32)
            for ri in range(2):
                for e in range(2):
                    at = ri * 8 + e * 4
                    row = turned[at:at + 1]
                    for p in range(1, 4):
                        row = jnp.where(path == p, turned[at + p:at + p + 1], row)
                    corr_out[ri, 0, e, o:o + 1, :] = row[:, 0:4]

    @pl.when(even)
    def _():
        lax.fori_loop(0, HALF - 2, z_block, 0)
        wait_halo_sends(0, HALF - 1)
        pl.semaphore_signal(go_sem, inc=1, device_id=dev(t_next, me), device_id_type=MESH)
        gather(0, 48)
        publish(0, 48)
        lax.fori_loop(HALF - 2, HALF, z_block, 0)
        finish_direction(2)
        spread(3, 1, 1)
        gather(1, 16)
        publish(1, 16)
        write_elementals()
        wait_halo_sends(HALF - 1, HALF)
        wait_bytes(taun.at[0], tau_sem.at[0])
        wait_bytes(taun.at[1], tau_sem.at[1])
        wait_bytes(rs_recv.at[0, :, pl.ds(0, 48)], rs_sem.at[0, 0])
        wait_bytes(rs_recv.at[1, :, pl.ds(0, 16)], rs_sem.at[1, 0])
        wait_bytes(ag.at[0, :, :, pl.ds(0, 48)], ag_sem.at[0, 0])
        wait_bytes(ag.at[1, :, :, pl.ds(0, 16)], ag_sem.at[1, 0])
        wait_bytes(ps_even, ps_sem.at[2])
        row = lax.broadcasted_iota(jnp.int32, (16, LANES), 0)
        first = ps_even[0, 0]
        second = ps_even[1, 0]
        for j in range(1, n_space):
            first = first + ps_even[0, j]
            second = second + ps_even[1, j]
        write_correlators(jnp.where(lax.rem(row, 8) < 4, first, second))

    @pl.when(odd)
    def _():
        pl.semaphore_wait(go_sem, 1)
        lax.fori_loop(0, HALF, start_halo, 0)
        gather(0, 48)
        lax.fori_loop(0, 2, z_block, 0)
        wait_bytes(taun.at[0], tau_sem.at[2])
        wait_bytes(taun.at[1], tau_sem.at[3])
        wait_bytes(tauo, local_sem.at[2])
        for e in range(2):
            for ri in range(2):
                taun[e, ri] = taun[e, ri].T
        wait_bytes(ag.at[0, :, :, pl.ds(0, 48)], ag_sem.at[0, 1])
        weights_of(0, 3, 0)
        lax.fori_loop(2, 5, z_block, 0)
        pair_rows((0, 1, 2), 0, 3)
        lax.fori_loop(5, HALF - 1, z_block, 0)
        wait_bytes(ag.at[1, :, :, pl.ds(0, 16)], ag_sem.at[1, 1])
        weights_of(1, 1, 3)
        pair_rows((0, 1, 2), 3, 4)
        lax.fori_loop(HALF - 1, HALF, z_block, 0)
        finish_direction(2)
        spread(3, 1, 1)
        pair_rows((3,), 0, 4)
        col = lax.broadcasted_iota(jnp.int32, (16, LANES), 1)
        for kind in range(2):
            tile = jnp.zeros((16, LANES), F32)
            for q in range(4):
                tile = jnp.where(col == q, jnp.sum(rowbuf[kind, q], axis=1, keepdims=True), tile)
            ps_send[kind] = tile

        def send_group(k, carry):
            remote(ps_send.at[0], ps_own.at[k - 1], ps_sem.at[0], ps_sem.at[1],
                   dev(t, lax.rem(me + k, n_space))).start()
            return carry

        def send_near(j, carry):
            remote(ps_send.at[1], ps_even.at[0, me], ps_sem.at[3], ps_sem.at[2], dev(t_next, j)).start()
            remote(ps_send.at[1], ps_even.at[1, me], ps_sem.at[3], ps_sem.at[2], dev(t_prev, j)).start()
            return carry

        lax.fori_loop(1, n_space, send_group, 0)
        lax.fori_loop(0, n_space, send_near, 0)
        gather(1, 16)
        write_elementals()
        wait_halo_sends(0, HALF)
        wait_bytes(rs_recv.at[0, :, pl.ds(0, 48)], rs_sem.at[0, 0])
        wait_bytes(rs_recv.at[1, :, pl.ds(0, 16)], rs_sem.at[1, 0])
        wait_bytes(ps_own, ps_sem.at[1])
        total = ps_send[0]
        for k in range(n_space - 1):
            total = total + ps_own[k]
        wait_bytes(ps_own, ps_sem.at[0])
        wait_bytes(ps_even, ps_sem.at[3])
        write_correlators(total)

    @pl.when(even)
    def _():
        wait_bytes(tauo, local_sem.at[2])


def solution(mesh):
    n_tm, n_space = mesh.shape["tm"], mesh.shape["space"]
    placed = (
        P("tm", None, None, None, "space"),
        P("tm", None, None, None, None, "space"),
        P("tm", None, None, None, None),
        P(),
        P(),
        P(),
    )

    def body(eigvecs, links, perambulators, directions, mom_pick, mom_table):
        hbm = pl.BlockSpec(memory_space=pl.ANY)
        smem = pl.BlockSpec(memory_space=pltpu.SMEM)
        vmem = pl.BlockSpec(memory_space=pltpu.VMEM)
        dma = pltpu.SemaphoreType.DMA
        return pl.pallas_call(
            functools.partial(kernel, n_tm, n_space),
            out_shape=(
                jax.ShapeDtypeStruct((4, 2, 1, ROWS, NV), F32),
                jax.ShapeDtypeStruct((2, 1, 2, 4, 4), F32),
            ),
            in_specs=[hbm, hbm, hbm, smem, smem, smem],
            out_specs=(vmem, vmem),
            scratch_shapes=[
                pltpu.VMEM((BLOCKS, 2, 3, NV, LANES), BF16),
                pltpu.VMEM((HALF, 2, 3, NV, LANES), BF16),
                pltpu.VMEM((HALF, 2, 3, NV, LANES), BF16),
                pltpu.VMEM((3, 2, 3, 3, BLOCKS * LANES), BF16),
                pltpu.VMEM((2, 3, 3, HALF * LANES), BF16),
                pltpu.VMEM((3, 2, 3, 3, BLOCKS * LANES), F32),
                pltpu.VMEM((2, 3, 3, HALF * LANES), F32),
                pltpu.VMEM((5, 2, 24, LANES), F32),
                pltpu.VMEM((512, 768), BF16),
                pltpu.VMEM((256, 768), BF16),
                pltpu.VMEM((256, 256), F32),
                pltpu.VMEM((3, 512, 256), F32),
                pltpu.VMEM((4, 2, NV, NV), F32),
                pltpu.VMEM((2, n_space, 48, NV), BF16),
                pltpu.VMEM((2, n_space - 1, 48, NV), BF16),
                pltpu.VMEM((2, 48, NV), F32),
                pltpu.VMEM((2, 48, NV), BF16),
                pltpu.VMEM((2, 2, n_space, 48, NV), BF16),
                pltpu.VMEM((2, 2, 512, 512), BF16),
                pltpu.VMEM((2, 2, 512, 512), BF16),
                pltpu.VMEM((2, 512, 512), BF16),
                pltpu.VMEM((2, 2, 4, 2, NV, NV), F32),
                pltpu.VMEM((2, 4, 16, NV), F32),
                pltpu.VMEM((2, 16, NV), F32),
                pltpu.VMEM((n_space - 1, 16, NV), F32),
                pltpu.VMEM((2, n_space, 16, NV), F32),
                dma((3,)),
                dma((2, HALF)),
                dma((2, HALF)),
                dma((2,)),
                dma((4,)),
                dma((2, 2)),
                dma((2, 2)),
                dma((4,)),
                pltpu.SemaphoreType.REGULAR,
            ],
            compiler_params=pltpu.CompilerParams(
                collective_id=0, has_side_effects=True, vmem_limit_bytes=48 << 20),
            name="elementals_and_correlators",
        )(eigvecs, links, perambulators, directions, mom_pick, mom_table)

    return jax.shard_map(
        body,
        mesh=mesh,
        in_specs=placed,
        out_specs=(P(None, None, "tm", "space", None), P(None, "tm", None, None, None)),
        check_vma=False,
    )
```

time: 424 us -> 103 us (0.24)
  the two profiles are of different devices: /device:TPU:2 before, /device:TPU:16 now
where the time goes in v1:
time: 103 us
  Pallas kernels  94.3 us (92%)
  local copies, waits for them, and re-layouts  7.95 us (8%)
    pallas_call x1, Pallas kernels, body(): pl.pallas_call(functools.partial(kernel, n_tm, n_space), out_shape=(jax.S...  94.3 us
    unnamed x12, local copies, waits for them, and re-layouts  7.95 us

profile of v1, /device:TPU:16, one launch (start us, length us, event | category | flops | bytes accessed | tf_op | source)
XLA Modules:
  0.0 102.9 jit_solution(13918600775970287884)
XLA Ops:
  0.6 0.8 copy.9.table
  1.4 1.1 %copy.8.links = bf16[1,3,2,3,3,2304]{5,4,3,2,1,0:T(4,128)(2,1)S(1)} copy(bf16[1,3,2,3,3,2304]{5,2,4,3,1,0:T(2,128)(2,1)} %param.7) | data formatting | bytes 497664 | tf_op args[1]
  2.5 0.0 copy-start
  2.5 2.0 %copy-done = bf16[1,2,3,128,2304]{4,3,2,1,0:T(8,128)(2,1)S(1)} copy-done((bf16[1,2,3,128,2304]{4,3,2,1,0:T(8,128)(2,1)S(1)}, bf16[1,2,3,128,2304]{4,3,2,1,0:T(8,128)(2,1)}, u32[]{:S(2)}) %copy-start) | copy-done | bytes 3538968
  4.5 0.0 copy-start.1
  4.5 1.6 %copy-done.1 = bf16[1,2,2,512,512]{4,3,2,1,0:T(8,128)(2,1)S(1)} copy-done((bf16[1,2,2,512,512]{4,3,2,1,0:T(8,128)(2,1)S(1)}, bf16[1,2,2,512,512]{4,3,2,1,0:T(8,128)(2,1)}, u32[]{:S(2)}) %copy-start.1) | copy-done | bytes 2097176
  6.1 0.0 copy-start.2
  6.1 0.7 copy-done.2
  6.7 0.0 copy-start.3
  6.7 0.7 copy-done.3
  7.4 94.3 %elementals_and_correlators.1 = (f32[4,2,1,8,128]{4,3,2,1,0:T(8,128)S(1)}, f32[2,1,2,4,4]{4,3,2,1,0:T(4,128)S(1)}) custom-call(bf16[1,2,3,128,2304]{4,3,2,1,0:T(8,128)(2,1)S(1)} %copy-done, bf16[1,3,2,3,3,2304]{5,4,3,2,1,0:T(4,128)(2,1)S(1)} %copy.8.links, bf16[1,2,2,512,512]{4,3,2,1,0:T(8,128)(2,1)S(1)} %copy-done.1, s32[4]{0:T(128)S(1)} %copy-done.2, ...), custom_call_target="tpu_custom_call" | custom-call | tf_op jit(solution)/shard_map/elementals_and_correlators/pallas_call | solution.py:539
  101.7 0.6 copy.12
  102.4 0.6 copy.13
Async XLA Ops:
  2.5 2.0 %copy-start = (bf16[1,2,3,128,2304]{4,3,2,1,0:T(8,128)(2,1)S(1)}, bf16[1,2,3,128,2304]{4,3,2,1,0:T(8,128)(2,1)}, u32[]{:S(2)}) copy-start(bf16[1,2,3,128,2304]{4,3,2,1,0:T(8,128)(2,1)} %eig.1) | copy-start | bytes 10616836
  4.5 1.6 %copy-start.1 = (bf16[1,2,2,512,512]{4,3,2,1,0:T(8,128)(2,1)S(1)}, bf16[1,2,2,512,512]{4,3,2,1,0:T(8,128)(2,1)}, u32[]{:S(2)}) copy-start(bf16[1,2,2,512,512]{4,3,2,1,0:T(8,128)(2,1)} %tau.1) | copy-start | bytes 6291460
  6.1 0.7 copy-start.2
  6.7 0.7 copy-start.3

commit v2 on v1

--- a/solution.py
+++ b/solution.py
@@ -25,7 +25,7 @@
 
 
 def kernel(n_tm, n_space, eig, links, tau, dirs, pick, table, elem_out, corr_out,
-           vbuf, rdn, rup, lk, lkup, lkf, lkupf, ph, lhs, rhs, acc0, accd, part,
+           vbuf, rdn, rup, lk, lkup, lkf, lkupf, ph, lhs, lhs2, lhsz, acc, accz, part,
            rs_send, rs_recv, own, ag_send, ag, tauo, taun, zbuf, wmat, rowbuf,
            ps_send, ps_own, ps_even, local_sem, halo_send, halo_recv, lk_sem, tau_sem,
            rs_sem, ag_sem, ps_sem, go_sem):
@@ -119,8 +119,8 @@
     for o in range(4):
         choice = spread_scalar(pick[o])
         row = [jnp.zeros((1, LANES), jnp.int32)] * 3
-        for r in range(table.shape[0]):
-            row = [jnp.where(choice == r, spread_scalar(table[r, axis]), row[axis]) for axis in range(3)]
+        for r in range(table.shape[1]):
+            row = [jnp.where(choice == r, spread_scalar(table[axis, r]), row[axis]) for axis in range(3)]
         picked.append(row)
 
     def path_momentum(path, axis):
@@ -132,58 +132,63 @@
     mom = [[path_momentum(path, axis) for axis in range(3)] for path in range(4)]
     extent_z = 1.0 * n_space
     plane = me.astype(F32)
-    for path in range(4):
-        flat = 2.0 * math.pi * (mom[path][0] * site_x / LXY + mom[path][1] * site_y / LXY
-                                + mom[path][2] * plane / extent_z)
-        ph[path, 0] = jnp.cos(flat)
-        ph[path, 1] = jnp.sin(flat)
-    flat = 2.0 * math.pi * (mom[3][0] * site_x / LXY + mom[3][1] * site_y / LXY
-                            + mom[3][2] * (plane - 1.0) / extent_z)
-    ph[4, 0] = jnp.cos(flat)
-    ph[4, 1] = jnp.sin(flat)
+    for slot, path, back in ((0, 0, (0, 0, 0)), (1, 1, (1, 0, 0)), (2, 2, (0, 1, 0)),
+                             (3, 3, (0, 0, 0)), (4, 3, (0, 0, 1))):
+        flat = 2.0 * math.pi * (mom[path][0] * (site_x - back[0]) / LXY
+                                + mom[path][1] * (site_y - back[1]) / LXY
+                                + mom[path][2] * (plane - back[2]) / extent_z)
+        ph[slot, 0] = jnp.cos(flat)
+        ph[slot, 1] = jnp.sin(flat)
 
     wait_bytes(lk, local_sem.at[1])
+    flat_x = lax.rem(lax.broadcasted_iota(jnp.int32, (2, BLOCKS * LANES), 1), LXY)
     for d in range(3):
-        for ri in range(2):
-            for c in range(3):
-                lkf[d, ri, c] = lk[d, ri, c].astype(F32)
+        for c in range(3):
+            for a in range(3):
+                pair = lk[d, c, a].astype(F32)
+                if d == 0:
+                    pair = jnp.where(flat_x == 0, pltpu.roll(pair, BLOCKS * LANES - LXY + 1, 1),
+                                     pltpu.roll(pair, 1, 1))
+                elif d == 1:
+                    pair = pltpu.roll(pair, LXY, 1)
+                at = (c * 3 + a) * 2
+                lkf[d, at:at + 2, :] = pair
     wait_bytes(vbuf, local_sem.at[0])
 
-    acc0[...] = jnp.zeros_like(acc0)
-    accd[...] = jnp.zeros_like(accd)
-    lane = lax.broadcasted_iota(jnp.int32, (NV, LANES), 1)
-
-    def link_rows(ref_row):
-        return [[[jnp.broadcast_to(ref_row(ri, c, a), (16, LANES)) for a in range(3)]
-                 for c in range(3)] for ri in range(2)]
-
-    def back_block(vref, u, cosine, sine, slot):
-        cosine = jnp.broadcast_to(cosine, (16, LANES))
-        sine = jnp.broadcast_to(sine, (16, LANES))
+    acc[...] = jnp.zeros_like(acc)
+    accz[...] = jnp.zeros_like(accz)
+    lane = lax.broadcasted_iota(jnp.int32, (16, LANES), 1)
+
+    def link_rows(ref, at):
+        return [[[jnp.broadcast_to(ref[pl.ds((c * 3 + a) * 2 + ri, 1), at], (8, LANES))
+                  for a in range(3)] for c in range(3)] for ri in range(2)]
+
+    def back_block(load, u, slot, j, dst, row, col):
+        cosine = jnp.broadcast_to(ph[slot, 0, pl.ds(j, 1), :], (8, LANES))
+        sine = jnp.broadcast_to(ph[slot, 1, pl.ds(j, 1), :], (8, LANES))
 
         def tile(k, carry):
             at = pl.multiple_of(k * 16, 16)
-            v = [[vref[ri, c, pl.ds(at, 16), :].astype(F32) for c in range(3)] for ri in range(2)]
+            v = [[load(ri, c, pl.ds(at, 16)) for c in range(3)] for ri in range(2)]
             for a in range(3):
-                b_re = u[0][0][a] * v[0][0] + u[1][0][a] * v[1][0]
-                b_im = u[0][0][a] * v[1][0] - u[1][0][a] * v[0][0]
-                for c in (1, 2):
-                    b_re = b_re + u[0][c][a] * v[0][c] + u[1][c][a] * v[1][c]
-                    b_im = b_im + u[0][c][a] * v[1][c] - u[1][c][a] * v[0][c]
-                col = pl.ds((slot * 3 + a) * LANES, LANES)
-                lhs[pl.ds(at, 16), col] = (cosine * b_re).astype(BF16)
-                lhs[pl.ds(at + 128, 16), col] = (cosine * b_im).astype(BF16)
-                lhs[pl.ds(at + 256, 16), col] = (sine * b_re).astype(BF16)
-                lhs[pl.ds(at + 384, 16), col] = (sine * b_im).astype(BF16)
-            return carry
-
-        lax.fori_loop(0, NV // 16, tile, 0, unroll=2)
-
-    def own_links(d, j):
-        at = pl.ds(pl.multiple_of(j * LANES, LANES), LANES)
-        return link_rows(lambda ri, c, a: lkf[d, ri, c, a:a + 1, at])
-
-    def plain_block(j, slot):
+                halves = []
+                for h in range(2):
+                    w = [[v[ri][c][h * 8:h * 8 + 8] for c in range(3)] for ri in range(2)]
+                    b_re = u[0][0][a] * w[0][0] + u[1][0][a] * w[1][0]
+                    b_im = u[0][0][a] * w[1][0] - u[1][0][a] * w[0][0]
+                    for c in (1, 2):
+                        b_re = b_re + u[0][c][a] * w[0][c] + u[1][c][a] * w[1][c]
+                        b_im = b_im + u[0][c][a] * w[1][c] - u[1][c][a] * w[0][c]
+                    halves.append((cosine * b_re, cosine * b_im, sine * b_re, sine * b_im))
+                lanes = pl.ds((col * 3 + a) * LANES, LANES)
+                for i in range(4):
+                    dst[pl.ds(at + row + i * 128, 16), lanes] = jnp.concatenate(
+                        [halves[0][i], halves[1][i]], axis=0).astype(BF16)
+            return carry
+
+        lax.fori_loop(0, NV // 16, tile, 0, unroll=True)
+
+    def plain_block(j, dst, col):
         cosine = jnp.broadcast_to(ph[0, 0, pl.ds(j, 1), :], (16, LANES))
         sine = jnp.broadcast_to(ph[0, 1, pl.ds(j, 1), :], (16, LANES))
 
@@ -192,53 +197,55 @@
             for c in range(3):
                 v_re = vbuf[j, 0, c, pl.ds(at, 16), :].astype(F32)
                 v_im = vbuf[j, 1, c, pl.ds(at, 16), :].astype(F32)
-                col = pl.ds((slot * 3 + c) * LANES, LANES)
-                rhs[pl.ds(at, 16), col] = (cosine * v_re + sine * v_im).astype(BF16)
-                rhs[pl.ds(at + 128, 16), col] = (cosine * v_im - sine * v_re).astype(BF16)
-            return carry
-
-        lax.fori_loop(0, NV // 16, tile, 0, unroll=2)
-
-    def ahead_block(d, j, slot):
-        after = jnp.where(j == BLOCKS - 1, 0, j + 1)
-        before = jnp.where(j == 0, BLOCKS - 1, j - 1)
-        if d == 0:
-            edge = lax.rem(j * LANES + lane, LXY) == LXY - 1
-        for ri in range(2):
-            for c in range(3):
-                here = vbuf[j, ri, c]
-                there = vbuf[after, ri, c]
-                if d == 1:
-                    turned = jnp.where(lane < LANES - LXY, pltpu.roll(here, LANES - LXY, 1),
-                                       pltpu.roll(there, LANES - LXY, 1))
-                else:
-                    back = vbuf[before, ri, c]
-                    near = jnp.where(lane == LANES - 1, pltpu.roll(there, LANES - 1, 1),
-                                     pltpu.roll(here, LANES - 1, 1))
-                    far = jnp.where(lane < LXY - 1, pltpu.roll(back, LXY - 1, 1),
-                                    pltpu.roll(here, LXY - 1, 1))
-                    turned = jnp.where(edge, far, near)
-                rhs[pl.ds(ri * 128, 128), pl.ds((slot * 3 + c) * LANES, LANES)] = turned
+                lanes = pl.ds((col * 3 + c) * LANES, LANES)
+                dst[pl.ds(at, 16), lanes] = (cosine * v_re + sine * v_im).astype(BF16)
+                dst[pl.ds(at + 128, 16), lanes] = (cosine * v_im - sine * v_re).astype(BF16)
+            return carry
+
+        lax.fori_loop(0, NV // 16, tile, 0, unroll=True)
 
     def stacked(parts):
         return jnp.concatenate(
             [jnp.concatenate([p[ri, c] for p in parts for c in range(3)], axis=1) for ri in range(2)],
             axis=0)
 
-    def local_pair(i, carry):
-        j = 2 * i
+    def fill(i, dst):
         for s in range(2):
-            plain_block(j + s, s)
-        acc0[...] += dot_nt(stacked([vbuf.at[j], vbuf.at[j + 1]]), rhs[...])
-        for d in range(2):
-            for s in range(2):
-                back_block(vbuf.at[j + s], own_links(d, j + s), ph[d + 1, 0, pl.ds(j + s, 1), :],
-                           ph[d + 1, 1, pl.ds(j + s, 1), :], s)
-                ahead_block(d, j + s, s)
-            accd[d] += dot_nt(lhs[...], rhs[...])
+            j = 2 * i + s
+            after = jnp.where(j == BLOCKS - 1, 0, j + 1)
+            before = jnp.where(j == 0, BLOCKS - 1, j - 1)
+            at = pl.ds(pl.multiple_of(j * LANES, LANES), LANES)
+            plain_block(j, dst, s)
+            first = lax.rem(j * LANES + lane, LXY) == 0
+
+            def from_x(ri, c, rows):
+                here = vbuf[j, ri, c, rows, :].astype(F32)
+                near = jnp.where(lane == LANES - 1, vbuf[before, ri, c, rows, :].astype(F32), here)
+                far = jnp.where(lane < LXY - 1, vbuf[after, ri, c, rows, :].astype(F32), here)
+                return jnp.where(first, pltpu.roll(far, LANES - LXY + 1, 1), pltpu.roll(near, 1, 1))
+
+            def from_y(ri, c, rows):
+                return pltpu.roll(jnp.where(lane >= LANES - LXY, vbuf[before, ri, c, rows, :].astype(F32),
+                                            vbuf[j, ri, c, rows, :].astype(F32)), LXY, 1)
+
+            back_block(from_x, link_rows(lkf.at[0], at), 1, j, dst, 256, s)
+            back_block(from_y, link_rows(lkf.at[1], at), 2, j, dst, 768, s)
+
+    def add_dot(i, src):
+        acc[...] += dot_nt(src[...], stacked([vbuf.at[2 * i], vbuf.at[2 * i + 1]]))
+
+    def two_pairs(i, carry):
+        fill(2 * i, lhs)
+        add_dot(jnp.maximum(2 * i - 1, 0), lhs2)
+        fill(2 * i + 1, lhs2)
+        add_dot(2 * i, lhs)
         return carry
 
-    lax.fori_loop(0, BLOCKS // 2, local_pair, 0)
+    lhs2[...] = jnp.zeros_like(lhs2)
+    lax.fori_loop(0, BLOCKS // 4, two_pairs, 0)
+    fill(BLOCKS // 2 - 1, lhs)
+    add_dot(BLOCKS // 2 - 2, lhs2)
+    add_dot(BLOCKS // 2 - 1, lhs)
 
     def blocks_of(ref, row):
         g_rr = ref[row:row + 128, 0:128]
@@ -248,8 +255,9 @@
         return g_rr + g_ii, g_ri - g_ir
 
     def finish_direction(d):
-        c_re, c_im = blocks_of(accd.at[d], 0)
-        s_re, s_im = blocks_of(accd.at[d], 256)
+        sums, row = (accz, 0) if d == 2 else (acc, 256 + 512 * d)
+        c_re, c_im = blocks_of(sums, row)
+        s_re, s_im = blocks_of(sums, row + 256)
         length = (float(LXY), float(LXY), extent_z)[d]
         turn = jnp.full((1, LANES), 2.0 * math.pi / length, F32) * mom[d + 1][d]
         cosine = jnp.cos(turn)
@@ -261,7 +269,9 @@
         part[d + 1, 0] = c_re + s_im - n_re.T
         part[d + 1, 1] = c_im - s_re + n_im.T
 
-    part[0, 0], part[0, 1] = blocks_of(acc0, 0)
+    plain_re, plain_im = blocks_of(acc, 0)
+    part[0, 0] = plain_re.T
+    part[0, 1] = -plain_im.T
     finish_direction(0)
     finish_direction(1)
 
@@ -307,19 +317,19 @@
     spread(0, 3, 0)
 
     link_copy.wait()
-    for ri in range(2):
-        for c in range(3):
-            lkupf[ri, c] = lkup[ri, c].astype(F32)
+    for c in range(3):
+        for a in range(3):
+            at = (c * 3 + a) * 2
+            lkupf[at:at + 2, :] = lkup[c, a].astype(F32)
 
     def z_block(n, carry):
         halo(n, 0).wait_recv()
         halo(n, 1).wait_recv()
         at = pl.ds(pl.multiple_of(n * LANES, LANES), LANES)
-        back_block(vbuf.at[n], own_links(2, n), ph[3, 0, pl.ds(n, 1), :], ph[3, 1, pl.ds(n, 1), :], 0)
-        u = link_rows(lambda ri, c, a: lkupf[ri, c, a:a + 1, at])
         m = n + HALF
-        back_block(rup.at[n], u, ph[4, 0, pl.ds(m, 1), :], ph[4, 1, pl.ds(m, 1), :], 1)
-        accd[2] += dot_nt(lhs[...], stacked([rdn.at[n], vbuf.at[m]]))
+        back_block(lambda ri, c, rows: vbuf[n, ri, c, rows, :].astype(F32), link_rows(lkf.at[2], at), 3, n, lhsz, 0, 0)
+        back_block(lambda ri, c, rows: rup[n, ri, c, rows, :].astype(F32), link_rows(lkupf, at), 4, m, lhsz, 0, 1)
+        accz[...] += dot_nt(lhsz[...], stacked([rdn.at[n], vbuf.at[m]]))
         return carry
 
     def wait_halo_sends(lo, hi):
@@ -330,61 +340,52 @@
 
         lax.fori_loop(lo, hi, one, 0)
 
-    def weights(kind, e, which, slot, path):
-        src = 0 if e == 0 else 1
-        if kind == 1:
-            src = 1 - e
-        re_rows, im_rows = [], []
-        at = pl.multiple_of(slot * 16, 16)
-        for j in range(n_space):
-            both = ag[which, src, j, pl.ds(at, 16), :].astype(F32)
-            re_rows.append(both[0:8])
-            im_rows.append(both[8:16])
-        phi_re = jnp.concatenate(re_rows, axis=0)
-        phi_im = jnp.concatenate(im_rows, axis=0)
-        if kind == 0:
-            first = jnp.concatenate([phi_re, phi_im], axis=1)
-            second = jnp.concatenate([phi_im, -phi_re], axis=1)
-        else:
-            first = jnp.concatenate([phi_re, -phi_im], axis=1)
-            second = jnp.concatenate([phi_im, phi_re], axis=1)
-        phi = jnp.concatenate([first, second], axis=0).astype(BF16)
+    def weights(kind, e, which, count, first_path):
+        src = e if kind == 0 else 1 - e
+        rows = []
+        for p in range(count):
+            both = [ag[which, src, j, pl.ds(p * 16, 16), :].astype(F32) for j in range(n_space)]
+            phi_re = jnp.concatenate([x[0:8] for x in both], axis=0)
+            phi_im = jnp.concatenate([x[8:16] for x in both], axis=0)
+            if kind == 0:
+                rows += [jnp.concatenate([phi_re, phi_im], axis=1), jnp.concatenate([phi_im, -phi_re], axis=1)]
+            else:
+                rows += [jnp.concatenate([phi_re, -phi_im], axis=1), jnp.concatenate([phi_im, phi_re], axis=1)]
+        phi = jnp.concatenate(rows, axis=0).astype(BF16)
         mat = tauo.at[e] if kind == 0 else taun.at[e]
         for c in range(4):
             col = slice(c * 128, (c + 1) * 128)
             z = dot_nt(jnp.concatenate([mat[0, :, col], mat[1, :, col]], axis=1), phi)
             if kind == 1 and c >= 2:
                 z = -z
-            zbuf[0, :, col] = z[:, 0:128].astype(BF16)
-            zbuf[1, :, col] = z[:, 128:256].astype(BF16)
+            z = z.astype(BF16)
+            for r in range(4):
+                for p in range(2 * count):
+                    zbuf[r, p * 128:(p + 1) * 128, col] = z[r * 128:(r + 1) * 128, p * 128:(p + 1) * 128]
         total = None
         for r in range(4):
             row = slice(r * 128, (r + 1) * 128)
-            g = dot_nt(jnp.concatenate([zbuf[0, row, :], zbuf[1, row, :]], axis=0),
-                       jnp.concatenate([mat[0, row, :], mat[1, row, :]], axis=0))
+            g = dot_nt(zbuf[r, 0:256 * count, :], jnp.concatenate([mat[0, row, :], mat[1, row, :]], axis=0))
             if total is None:
                 total = g
             elif kind == 0 and r >= 2:
                 total = total - g
             else:
                 total = total + g
-        rr, ri_, ir, ii = (total[0:128, 0:128], total[0:128, 128:256],
-                           total[128:256, 0:128], total[128:256, 128:256])
-        if kind == 0:
-            wmat[kind, e, path, 0] = rr - ii
-            wmat[kind, e, path, 1] = ri_ + ir
-        else:
-            wmat[kind, e, path, 0] = rr + ii
-            wmat[kind, e, path, 1] = ir - ri_
-
-    def weights_of(which, count, first):
+        for p in range(count):
+            one = total[p * 256:(p + 1) * 256]
+            rr, ri_, ir, ii = one[0:128, 0:128], one[0:128, 128:256], one[128:256, 0:128], one[128:256, 128:256]
+            if kind == 0:
+                wmat[kind, e, first_path + p, 0] = rr - ii
+                wmat[kind, e, first_path + p, 1] = ri_ + ir
+            else:
+                wmat[kind, e, first_path + p, 0] = rr + ii
+                wmat[kind, e, first_path + p, 1] = ir - ri_
+
+    def weights_of(which, count, first_path):
         for kind in range(2):
             for e in range(2):
-                def one(slot, carry, kind=kind, e=e):
-                    weights(kind, e, which, slot, first + slot)
-                    return carry
-
-                lax.fori_loop(0, count, one, 0)
+                weights(kind, e, which, count, first_path)
 
     def pair_rows(paths, lo, hi):
         for kind in range(2):
@@ -548,15 +549,16 @@
                 pltpu.VMEM((BLOCKS, 2, 3, NV, LANES), BF16),
                 pltpu.VMEM((HALF, 2, 3, NV, LANES), BF16),
                 pltpu.VMEM((HALF, 2, 3, NV, LANES), BF16),
-                pltpu.VMEM((3, 2, 3, 3, BLOCKS * LANES), BF16),
-                pltpu.VMEM((2, 3, 3, HALF * LANES), BF16),
-                pltpu.VMEM((3, 2, 3, 3, BLOCKS * LANES), F32),
-                pltpu.VMEM((2, 3, 3, HALF * LANES), F32),
+                pltpu.VMEM((3, 3, 3, 2, BLOCKS * LANES), BF16),
+                pltpu.VMEM((3, 3, 2, HALF * LANES), BF16),
+                pltpu.VMEM((3, 24, BLOCKS * LANES), F32),
+                pltpu.VMEM((24, HALF * LANES), F32),
                 pltpu.VMEM((5, 2, 24, LANES), F32),
+                pltpu.VMEM((1280, 768), BF16),
+                pltpu.VMEM((1280, 768), BF16),
                 pltpu.VMEM((512, 768), BF16),
-                pltpu.VMEM((256, 768), BF16),
-                pltpu.VMEM((256, 256), F32),
-                pltpu.VMEM((3, 512, 256), F32),
+                pltpu.VMEM((1280, 256), F32),
+                pltpu.VMEM((512, 256), F32),
                 pltpu.VMEM((4, 2, NV, NV), F32),
                 pltpu.VMEM((2, n_space, 48, NV), BF16),
                 pltpu.VMEM((2, n_space - 1, 48, NV), BF16),
@@ -565,7 +567,7 @@
                 pltpu.VMEM((2, 2, n_space, 48, NV), BF16),
                 pltpu.VMEM((2, 2, 512, 512), BF16),
                 pltpu.VMEM((2, 2, 512, 512), BF16),
-                pltpu.VMEM((2, 512, 512), BF16),
+                pltpu.VMEM((4, 768, 512), BF16),
                 pltpu.VMEM((2, 2, 4, 2, NV, NV), F32),
                 pltpu.VMEM((2, 4, 16, NV), F32),
                 pltpu.VMEM((2, 16, NV), F32),
@@ -582,9 +584,10 @@
                 pltpu.SemaphoreType.REGULAR,
             ],
             compiler_params=pltpu.CompilerParams(
-                collective_id=0, has_side_effects=True, vmem_limit_bytes=48 << 20),
+                collective_id=0, has_side_effects=True, vmem_limit_bytes=60 << 20),
             name="elementals_and_correlators",
-        )(eigvecs, links, perambulators, directions, mom_pick, mom_table)
+        )(eigvecs, jnp.transpose(links, (0, 1, 3, 4, 2, 5)), perambulators, directions, mom_pick,
+          mom_table.T)
 
     return jax.shard_map(
         body,

time: 103 us -> 95 us (0.922)
  local copies, waits for them, and re-layouts: 7.95 us -> 2.67 us
  Pallas kernels: 94.3 us -> 91.5 us
    unnamed x12 -> x2, local copies, waits for them, and re-layouts: 7.95 us -> 2.67 us
    pallas_call x1, Pallas kernels: 94.3 us -> 91.5 us  [body(): pl.pallas_call(functools.partial(kernel, n_tm, n_space), out_shape=(jax.S...]
where the time goes in v2:
time: 95 us; the launch traced here: 94.8 us
  Pallas kernels  91.5 us (96%)
  local copies, waits for them, and re-layouts  2.67 us (3%)
    pallas_call x1, Pallas kernels, body(): pl.pallas_call(functools.partial(kernel, n_tm, n_space), out_shape=(jax.S...  91.5 us
    unnamed x2, local copies, waits for them, and re-layouts  2.67 us

profile of v2, /device:TPU:16, one launch (start us, length us, event | category | flops | bytes accessed | tf_op | source)
XLA Modules:
  0.0 94.8 jit_solution(16062780716344896325)
XLA Ops:
  0.6 91.5 %elementals_and_correlators.1 = (f32[4,2,1,8,128]{4,3,2,1,0:T(8,128)}, f32[2,1,2,4,4]{4,3,2,1,0:T(4,128)}) custom-call(bf16[1,2,3,128,2304]{4,3,2,1,0:T(8,128)(2,1)} %eig.1, bf16[1,3,3,3,2,2304]{5,4,3,2,1,0:T(2,128)(2,1)} %bitcast.2, bf16[1,2,2,512,512]{4,3,2,1,0:T(8,128)(2,1)} %tau.1, s32[4]{0:T(128)} %dirs.1, s32[4]{0:T(128)} %pick.1, s32[3,7]{1,0:T(4,128)} %bitcast.3), custom_call_target="tpu_custom_call" | custom-call | tf_op jit(solution)/shard_map/elementals_and_correlators/pallas_call | solution.py:540
  92.1 1.4 %copy.10 = f32[4,2,1,8,128]{4,3,2,1,0:T(8,128)} copy(f32[4,2,1,8,128]{4,3,2,1,0:T(8,128)} %get-tuple-element.4) | data formatting | bytes 65536
  93.5 1.3 %copy.11 = f32[2,1,2,4,4]{4,3,2,1,0:T(4,128)} copy(f32[2,1,2,4,4]{4,3,2,1,0:T(4,128)} %get-tuple-element.5) | data formatting | bytes 512

commit v3 on v2

--- a/solution.py
+++ b/solution.py
@@ -27,8 +27,8 @@
 def kernel(n_tm, n_space, eig, links, tau, dirs, pick, table, elem_out, corr_out,
            vbuf, rdn, rup, lk, lkup, lkf, lkupf, ph, lhs, lhs2, lhsz, acc, accz, part,
            rs_send, rs_recv, own, ag_send, ag, tauo, taun, zbuf, wmat, rowbuf,
-           ps_send, ps_own, ps_even, local_sem, halo_send, halo_recv, lk_sem, tau_sem,
-           rs_sem, ag_sem, ps_sem, go_sem):
+           ysend, yrecv, ps_send, ps_own, ps_even, local_sem, halo_send, halo_recv, lk_sem,
+           rs_sem, ag_sem, fw_sem, y_sem, ps_sem, go_sem):
     t = lax.axis_index("tm")
     me = lax.axis_index("space")
     odd = lax.rem(t, 2) == 1
@@ -104,8 +104,6 @@
     @pl.when(even)
     def _():
         lax.fori_loop(0, HALF, start_halo, 0)
-        remote(tau.at[0, 0], taun.at[0], tau_sem.at[0], tau_sem.at[2], dev(t_prev, me)).start()
-        remote(tau.at[0, 1], taun.at[1], tau_sem.at[1], tau_sem.at[3], dev(t_next, me)).start()
 
     site = (lax.broadcasted_iota(jnp.int32, (24, LANES), 0) * LANES
             + lax.broadcasted_iota(jnp.int32, (24, LANES), 1)).astype(F32)
@@ -304,17 +302,36 @@
 
     def publish(which, width):
         ag_send[which, 0:width, :] = own[which, 0:width, :].astype(BF16)
-
-        def send(j, carry):
+        ag[which, 0, me, 0:width, :] = ag_send[which, 0:width, :]
+
+        def send(k, carry):
             remote(ag_send.at[which, pl.ds(0, width)], ag.at[which, 0, me, pl.ds(0, width)],
-                   ag_sem.at[which, 0], ag_sem.at[which, 1], dev(t_next, j)).start()
-            remote(ag_send.at[which, pl.ds(0, width)], ag.at[which, 1, me, pl.ds(0, width)],
-                   ag_sem.at[which, 0], ag_sem.at[which, 1], dev(t_prev, j)).start()
+                   ag_sem.at[which, 0], ag_sem.at[which, 1],
+                   dev(t, lax.rem(me + k, n_space))).start()
             return carry
 
-        lax.fori_loop(0, n_space, send, 0)
-
-    spread(0, 3, 0)
+        lax.fori_loop(1, n_space, send, 0)
+
+    def forward(which, width):
+        wait_bytes(ag.at[which, 0, pl.ds(0, n_space - 1), pl.ds(0, width)], ag_sem.at[which, 1])
+        for side, where in ((0, t_next), (1, t_prev)):
+            remote(ag.at[which, 0, :, pl.ds(0, width)], ag.at[which, side, :, pl.ds(0, width)],
+                   fw_sem.at[which, side], fw_sem.at[which, 2], dev(where, me)).start()
+
+    def send_weights(which, first_path, count):
+        for e, where in ((0, t_prev), (1, t_next)):
+            paths = pl.ds(first_path, count)
+            remote(ysend.at[e, paths], yrecv.at[e, paths], y_sem.at[which, 0, e], y_sem.at[which, 1, e],
+                   dev(where, me)).start()
+
+    def wait_weights(which, first_path, count, side):
+        for e in range(2):
+            wait_bytes(yrecv.at[e, pl.ds(first_path, count)], y_sem.at[which, side, e])
+
+    @pl.when(even)
+    def _():
+        spread(0, 3, 0)
+
 
     link_copy.wait()
     for c in range(3):
@@ -341,7 +358,7 @@
         lax.fori_loop(lo, hi, one, 0)
 
     def weights(kind, e, which, count, first_path):
-        src = e if kind == 0 else 1 - e
+        src = e if kind == 0 else 0
         rows = []
         for p in range(count):
             both = [ag[which, src, j, pl.ds(p * 16, 16), :].astype(F32) for j in range(n_space)]
@@ -376,35 +393,34 @@
             one = total[p * 256:(p + 1) * 256]
             rr, ri_, ir, ii = one[0:128, 0:128], one[0:128, 128:256], one[128:256, 0:128], one[128:256, 128:256]
             if kind == 0:
-                wmat[kind, e, first_path + p, 0] = rr - ii
-                wmat[kind, e, first_path + p, 1] = ri_ + ir
+                wmat[e, first_path + p, 0] = rr - ii
+                wmat[e, first_path + p, 1] = ri_ + ir
             else:
-                wmat[kind, e, first_path + p, 0] = rr + ii
-                wmat[kind, e, first_path + p, 1] = ir - ri_
-
-    def weights_of(which, count, first_path):
-        for kind in range(2):
-            for e in range(2):
-                weights(kind, e, which, count, first_path)
-
-    def pair_rows(paths, lo, hi):
-        for kind in range(2):
-            for e in range(2):
-                for p in paths:
-                    def one(w, carry, kind=kind, e=e, p=p):
-                        w_re, w_im = wmat[kind, e, w, 0], wmat[kind, e, w, 1]
-                        p_re, p_im = part[p, 0], part[p, 1]
-                        re = jnp.sum(p_re * w_re - p_im * w_im, axis=0, keepdims=True)
-                        im = jnp.sum(p_re * w_im + p_im * w_re, axis=0, keepdims=True)
-                        if kind == 0:
-                            rowbuf[kind, w, pl.ds(e * 4 + p, 1), :] = re
-                            rowbuf[kind, w, pl.ds(8 + e * 4 + p, 1), :] = im
-                        else:
-                            rowbuf[kind, p, pl.ds(e * 4 + w, 1), :] = re
-                            rowbuf[kind, p, pl.ds(8 + e * 4 + w, 1), :] = im
-                        return carry
-
-                    lax.fori_loop(lo, hi, one, 0)
+                ysend[e, first_path + p, 0] = (rr + ii).astype(BF16)
+                ysend[e, first_path + p, 1] = (ir - ri_).astype(BF16)
+
+    def weights_of(kind, which, count, first_path):
+        for e in range(2):
+            weights(kind, e, which, count, first_path)
+
+    def pair_rows(kind, paths, lo, hi):
+        mat = wmat if kind == 0 else yrecv
+        for e in range(2):
+            for p in paths:
+                def one(w, carry, e=e, p=p):
+                    w_re, w_im = mat[e, w, 0].astype(F32), mat[e, w, 1].astype(F32)
+                    p_re, p_im = part[p, 0], part[p, 1]
+                    re = jnp.sum(p_re * w_re - p_im * w_im, axis=0, keepdims=True)
+                    im = jnp.sum(p_re * w_im + p_im * w_re, axis=0, keepdims=True)
+                    if kind == 0:
+                        rowbuf[kind, w, pl.ds(e * 4 + p, 1), :] = re
+                        rowbuf[kind, w, pl.ds(8 + e * 4 + p, 1), :] = im
+                    else:
+                        rowbuf[kind, p, pl.ds(e * 4 + w, 1), :] = re
+                        rowbuf[kind, p, pl.ds(8 + e * 4 + w, 1), :] = im
+                    return carry
+
+                lax.fori_loop(lo, hi, one, 0)
 
     def write_elementals():
         for o in range(4):
@@ -433,24 +449,36 @@
 
     @pl.when(even)
     def _():
-        lax.fori_loop(0, HALF - 2, z_block, 0)
-        wait_halo_sends(0, HALF - 1)
+        lax.fori_loop(0, 4, z_block, 0)
+        wait_halo_sends(0, 5)
         pl.semaphore_signal(go_sem, inc=1, device_id=dev(t_next, me), device_id_type=MESH)
+        lax.fori_loop(4, HALF, z_block, 0)
+        finish_direction(2)
+        spread(3, 1, 1)
         gather(0, 48)
         publish(0, 48)
-        lax.fori_loop(HALF - 2, HALF, z_block, 0)
-        finish_direction(2)
-        spread(3, 1, 1)
+        wait_bytes(tauo, local_sem.at[2])
+        for e in range(2):
+            for ri in range(2):
+                taun[e, ri] = tauo[e, ri].T
         gather(1, 16)
         publish(1, 16)
+        forward(0, 48)
+        weights_of(1, 0, 3, 0)
+        send_weights(0, 0, 3)
+        forward(1, 16)
+        weights_of(1, 1, 1, 3)
+        send_weights(1, 3, 1)
         write_elementals()
-        wait_halo_sends(HALF - 1, HALF)
-        wait_bytes(taun.at[0], tau_sem.at[0])
-        wait_bytes(taun.at[1], tau_sem.at[1])
+        wait_halo_sends(5, HALF)
         wait_bytes(rs_recv.at[0, :, pl.ds(0, 48)], rs_sem.at[0, 0])
         wait_bytes(rs_recv.at[1, :, pl.ds(0, 16)], rs_sem.at[1, 0])
-        wait_bytes(ag.at[0, :, :, pl.ds(0, 48)], ag_sem.at[0, 0])
-        wait_bytes(ag.at[1, :, :, pl.ds(0, 16)], ag_sem.at[1, 0])
+        for which, width in ((0, 48), (1, 16)):
+            wait_bytes(ag.at[which, 0, pl.ds(0, n_space - 1), pl.ds(0, width)], ag_sem.at[which, 0])
+            for side in range(2):
+                wait_bytes(ag.at[which, 0, :, pl.ds(0, width)], fw_sem.at[which, side])
+        wait_weights(0, 0, 3, 0)
+        wait_weights(1, 3, 1, 0)
         wait_bytes(ps_even, ps_sem.at[2])
         row = lax.broadcasted_iota(jnp.int32, (16, LANES), 0)
         first = ps_even[0, 0]
@@ -464,26 +492,23 @@
     def _():
         pl.semaphore_wait(go_sem, 1)
         lax.fori_loop(0, HALF, start_halo, 0)
-        gather(0, 48)
-        lax.fori_loop(0, 2, z_block, 0)
-        wait_bytes(taun.at[0], tau_sem.at[2])
-        wait_bytes(taun.at[1], tau_sem.at[3])
+        lax.fori_loop(0, 7, z_block, 0)
         wait_bytes(tauo, local_sem.at[2])
-        for e in range(2):
-            for ri in range(2):
-                taun[e, ri] = taun[e, ri].T
-        wait_bytes(ag.at[0, :, :, pl.ds(0, 48)], ag_sem.at[0, 1])
-        weights_of(0, 3, 0)
-        lax.fori_loop(2, 5, z_block, 0)
-        pair_rows((0, 1, 2), 0, 3)
-        lax.fori_loop(5, HALF - 1, z_block, 0)
-        wait_bytes(ag.at[1, :, :, pl.ds(0, 16)], ag_sem.at[1, 1])
-        weights_of(1, 1, 3)
-        pair_rows((0, 1, 2), 3, 4)
-        lax.fori_loop(HALF - 1, HALF, z_block, 0)
+        wait_bytes(ag.at[0, :, :, pl.ds(0, 48)], fw_sem.at[0, 2])
+        weights_of(0, 0, 3, 0)
+        pair_rows(0, (0, 1, 2), 0, 3)
+        lax.fori_loop(7, HALF, z_block, 0)
         finish_direction(2)
         spread(3, 1, 1)
-        pair_rows((3,), 0, 4)
+        spread(0, 3, 0)
+        pair_rows(0, (3,), 0, 3)
+        wait_weights(0, 0, 3, 1)
+        pair_rows(1, (0, 1, 2, 3), 0, 3)
+        wait_bytes(ag.at[1, :, :, pl.ds(0, 16)], fw_sem.at[1, 2])
+        weights_of(0, 1, 1, 3)
+        pair_rows(0, (0, 1, 2, 3), 3, 4)
+        wait_weights(1, 3, 1, 1)
+        pair_rows(1, (0, 1, 2, 3), 3, 4)
         col = lax.broadcasted_iota(jnp.int32, (16, LANES), 1)
         for kind in range(2):
             tile = jnp.zeros((16, LANES), F32)
@@ -501,9 +526,10 @@
             remote(ps_send.at[1], ps_even.at[1, me], ps_sem.at[3], ps_sem.at[2], dev(t_prev, j)).start()
             return carry
 
+        lax.fori_loop(0, n_space, send_near, 0)
         lax.fori_loop(1, n_space, send_group, 0)
-        lax.fori_loop(0, n_space, send_near, 0)
         gather(1, 16)
+        gather(0, 48)
         write_elementals()
         wait_halo_sends(0, HALF)
         wait_bytes(rs_recv.at[0, :, pl.ds(0, 48)], rs_sem.at[0, 0])
@@ -515,10 +541,6 @@
         wait_bytes(ps_own, ps_sem.at[0])
         wait_bytes(ps_even, ps_sem.at[3])
         write_correlators(total)
-
-    @pl.when(even)
-    def _():
-        wait_bytes(tauo, local_sem.at[2])
 
 
 def solution(mesh):
@@ -568,8 +590,10 @@
                 pltpu.VMEM((2, 2, 512, 512), BF16),
                 pltpu.VMEM((2, 2, 512, 512), BF16),
                 pltpu.VMEM((4, 768, 512), BF16),
-                pltpu.VMEM((2, 2, 4, 2, NV, NV), F32),
+                pltpu.VMEM((2, 4, 2, NV, NV), F32),
                 pltpu.VMEM((2, 4, 16, NV), F32),
+                pltpu.VMEM((2, 4, 2, NV, NV), BF16),
+                pltpu.VMEM((2, 4, 2, NV, NV), BF16),
                 pltpu.VMEM((2, 16, NV), F32),
                 pltpu.VMEM((n_space - 1, 16, NV), F32),
                 pltpu.VMEM((2, n_space, 16, NV), F32),
@@ -577,9 +601,10 @@
                 dma((2, HALF)),
                 dma((2, HALF)),
                 dma((2,)),
-                dma((4,)),
                 dma((2, 2)),
                 dma((2, 2)),
+                dma((2, 3)),
+                dma((2, 2, 2)),
                 dma((4,)),
                 pltpu.SemaphoreType.REGULAR,
             ],

time: 95 us -> 79.6 us (0.84)
  Pallas kernels: 91.5 us -> 75.2 us
    pallas_call x1, Pallas kernels: 91.5 us -> 75.2 us  [body(): pl.pallas_call(functools.partial(kernel, n_tm, n_space), out_shape=(jax.S...]
where the time goes in v3:
time: 79.6 us; the launch traced here: 78.5 us
  Pallas kernels  75.2 us (94%)
  local copies, waits for them, and re-layouts  2.67 us (3%)
    pallas_call x1, Pallas kernels, body(): pl.pallas_call(functools.partial(kernel, n_tm, n_space), out_shape=(jax.S...  75.2 us
    unnamed x2, local copies, waits for them, and re-layouts  2.67 us

profile of v3, /device:TPU:16, one launch (start us, length us, event | category | flops | bytes accessed | tf_op | source)
XLA Modules:
  0.0 78.5 jit_solution(4606267860633954969)
XLA Ops:
  0.6 75.2 %elementals_and_correlators.1 = (f32[4,2,1,8,128]{4,3,2,1,0:T(8,128)}, f32[2,1,2,4,4]{4,3,2,1,0:T(4,128)}) custom-call(bf16[1,2,3,128,2304]{4,3,2,1,0:T(8,128)(2,1)} %eig.1, bf16[1,3,3,3,2,2304]{5,4,3,2,1,0:T(2,128)(2,1)} %bitcast.2, bf16[1,2,2,512,512]{4,3,2,1,0:T(8,128)(2,1)} %tau.1, s32[4]{0:T(128)} %dirs.1, s32[4]{0:T(128)} %pick.1, s32[3,7]{1,0:T(4,128)} %bitcast.3), custom_call_target="tpu_custom_call" | custom-call | tf_op jit(solution)/shard_map/elementals_and_correlators/pallas_call | solution.py:562
  75.8 1.4 %copy.10 = f32[4,2,1,8,128]{4,3,2,1,0:T(8,128)} copy(f32[4,2,1,8,128]{4,3,2,1,0:T(8,128)} %get-tuple-element.4) | data formatting | bytes 65536
  77.2 1.3 %copy.11 = f32[2,1,2,4,4]{4,3,2,1,0:T(4,128)} copy(f32[2,1,2,4,4]{4,3,2,1,0:T(4,128)} %get-tuple-element.5) | data formatting | bytes 512

commit v4 on v3

--- a/solution.py
+++ b/solution.py
@@ -54,15 +54,6 @@
             eig.at[0, :, :, :, pl.ds(pl.multiple_of(j * LANES, LANES), LANES)],
             vbuf.at[j], local_sem.at[0])
 
-    pltpu.make_async_copy(links.at[0], lk, local_sem.at[1]).start()
-
-    def start_load(j, carry):
-        load_block(j).start()
-        return carry
-
-    lax.fori_loop(0, BLOCKS, start_load, 0)
-    pltpu.make_async_copy(tau.at[0], tauo, local_sem.at[2]).start()
-
     barrier = pltpu.get_barrier_semaphore()
 
     def greet(a, b):
@@ -83,6 +74,15 @@
         return carry
 
     lax.fori_loop(0, n_space, greet_near, 0)
+    pltpu.make_async_copy(links.at[0], lk, local_sem.at[1]).start()
+
+    def start_load(j, carry):
+        load_block(j).start()
+        return carry
+
+    lax.fori_loop(0, BLOCKS, start_load, 0)
+    pltpu.make_async_copy(tau.at[0], tauo, local_sem.at[2]).start()
+
     pl.semaphore_wait(barrier, 3 * n_space - 1)
 
     def halo(n, side):
@@ -449,10 +449,9 @@
 
     @pl.when(even)
     def _():
-        lax.fori_loop(0, 4, z_block, 0)
-        wait_halo_sends(0, 5)
+        wait_halo_sends(0, 7)
         pl.semaphore_signal(go_sem, inc=1, device_id=dev(t_next, me), device_id_type=MESH)
-        lax.fori_loop(4, HALF, z_block, 0)
+        lax.fori_loop(0, HALF, z_block, 0)
         finish_direction(2)
         spread(3, 1, 1)
         gather(0, 48)
@@ -470,7 +469,7 @@
         weights_of(1, 1, 1, 3)
         send_weights(1, 3, 1)
         write_elementals()
-        wait_halo_sends(5, HALF)
+        wait_halo_sends(7, HALF)
         wait_bytes(rs_recv.at[0, :, pl.ds(0, 48)], rs_sem.at[0, 0])
         wait_bytes(rs_recv.at[1, :, pl.ds(0, 16)], rs_sem.at[1, 0])
         for which, width in ((0, 48), (1, 16)):

time: 79.6 us -> 78.8 us (0.990)
  Pallas kernels: 75.2 us -> 74.3 us
    pallas_call x1, Pallas kernels: 75.2 us -> 74.3 us  [body(): pl.pallas_call(functools.partial(kernel, n_tm, n_space), out_shape=(jax.S...]
where the time goes in v4:
time: 78.8 us; the launch traced here: 77.6 us
  Pallas kernels  74.3 us (94%)
  local copies, waits for them, and re-layouts  2.67 us (3%)
    pallas_call x1, Pallas kernels, body(): pl.pallas_call(functools.partial(kernel, n_tm, n_space), out_shape=(jax.S...  74.3 us
    unnamed x2, local copies, waits for them, and re-layouts  2.67 us

profile of v4, /device:TPU:16, one launch (start us, length us, event | category | flops | bytes accessed | tf_op | source)
XLA Modules:
  0.0 77.6 jit_solution(18368657231330897524)
XLA Ops:
  0.6 74.3 %elementals_and_correlators.1 = (f32[4,2,1,8,128]{4,3,2,1,0:T(8,128)}, f32[2,1,2,4,4]{4,3,2,1,0:T(4,128)}) custom-call(bf16[1,2,3,128,2304]{4,3,2,1,0:T(8,128)(2,1)} %eig.1, bf16[1,3,3,3,2,2304]{5,4,3,2,1,0:T(2,128)(2,1)} %bitcast.2, bf16[1,2,2,512,512]{4,3,2,1,0:T(8,128)(2,1)} %tau.1, s32[4]{0:T(128)} %dirs.1, s32[4]{0:T(128)} %pick.1, s32[3,7]{1,0:T(4,128)} %bitcast.3), custom_call_target="tpu_custom_call" | custom-call | tf_op jit(solution)/shard_map/elementals_and_correlators/pallas_call | solution.py:561
  75.0 1.4 %copy.10 = f32[4,2,1,8,128]{4,3,2,1,0:T(8,128)} copy(f32[4,2,1,8,128]{4,3,2,1,0:T(8,128)} %get-tuple-element.4) | data formatting | bytes 65536
  76.3 1.3 %copy.11 = f32[2,1,2,4,4]{4,3,2,1,0:T(4,128)} copy(f32[2,1,2,4,4]{4,3,2,1,0:T(4,128)} %get-tuple-element.5) | data formatting | bytes 512
